TPU v7x, 32 devices: a whole 2x2x4 slice. The times are simulated.
32 devices in a mesh: grp: 2 (over y), tm: 4 (over z), chan: 4 (over x, core).
Axes of the slice: x: 2, y: 2, z: 4, core: 2. Of those that a mesh axis runs over, the one named last changes fastest.
Arguments:
- voltages: int32 [512, 65536], P(('grp', 'chan'), 'tm'), parts along dimension 0, may hold values from -128 to 127
- beam_delays: int32 [256, 256], replicated, may hold values from 0 to 4095
- cal_gains: float32 [2, 4096, 256], P(None, ('grp', 'tm', 'chan')), parts along dimension 1, may hold values from -4 to 4
Outputs:
- visibilities: bfloat16 [2, 4096, 256, 256], P(None, ('grp', 'tm', 'chan')), parts along dimension 1
- beam_power: bfloat16 [4096, 16, 256], P(('grp', 'tm', 'chan')), parts along dimension 0
There are 2 independent parts, one for each index of `grp`. A program takes and returns all parts, laid end to end along the dimension named above; an argument that names none is the same for every part. Nothing has to cross between parts.
All inputs are finite; a program needn't handle non-finite values.
Results may differ from a plain program's by a relative error of at most 0.0062.
Values may be sent and summed in bfloat16 or wider, within the bound.
No kernel may reach another device: no remote copies, remote signals or barrier semaphores. Data moves between devices by JAX's collectives and lax.ppermute only.
A program may use at most 192 MiB of HBM per device.

v0:
```python
import math

import jax
import jax.numpy as jnp
from jax import lax
from jax.sharding import PartitionSpec as P

TAPS = 4
FA = 64
FB = 64
NFFT = 4096
CH = 2048


def shifted(block, axis, distance):
    devices = range(lax.axis_size(axis))
    route = [(i - distance, i) for i in devices if i - distance in devices]
    return lax.ppermute(block, axis, route)


def pfb_window():
    total_len = TAPS * NFFT
    sample_pos = jnp.arange(total_len, dtype=jnp.float32)
    centre = (sample_pos - total_len / 2 + 0.5) / NFFT
    taper_win = 0.5 - 0.5 * jnp.cos(2.0 * math.pi * (sample_pos + 0.5) / total_len)
    coeffs = jnp.sinc(centre) * taper_win
    coeffs = coeffs / jnp.sqrt(jnp.sum(coeffs * coeffs))
    return coeffs.reshape(TAPS, NFFT)


def phase_table(left, right, modulus):
    phase_idx = left[:, None] * right[None, :] % modulus
    angles = phase_idx.astype(jnp.float32) * (2.0 * math.pi / modulus)
    return (jnp.cos(angles), jnp.sin(angles))


def transform(row_block):
    best = lax.Precision.HIGHEST
    first_idx = jnp.arange(FA, dtype=jnp.int32)
    second_idx = jnp.arange(FB, dtype=jnp.int32)
    half_idx = jnp.arange(FB // 2, dtype=jnp.int32)
    cos_one, sin_one = phase_table(first_idx, first_idx, FA)
    section_re = jnp.einsum("rab,ak->rkb", row_block, cos_one, precision=best)
    section_im = -jnp.einsum("rab,ak->rkb", row_block, sin_one, precision=best)
    twid_cos, twid_sin = phase_table(first_idx, second_idx, NFFT)
    inner_re = section_re * twid_cos + section_im * twid_sin
    inner_im = section_im * twid_cos - section_re * twid_sin
    cos_two, sin_two = phase_table(second_idx, half_idx, FB)
    freq_re = jnp.einsum("rkb,bq->qkr", inner_re, cos_two, precision=best) + jnp.einsum(
        "rkb,bq->qkr", inner_im, sin_two, precision=best
    )
    freq_im = jnp.einsum("rkb,bq->qkr", inner_im, cos_two, precision=best) - jnp.einsum(
        "rkb,bq->qkr", inner_re, sin_two, precision=best
    )
    row_count = row_block.shape[0]
    return (freq_re.reshape(CH, row_count), freq_im.reshape(CH, row_count))


def shards(voltages, beam_delays, cal_gains):
    inp_dev = voltages.shape[0]
    spec_dev = voltages.shape[1] // NFFT
    tm_count = lax.axis_size("tm")
    chan_count = lax.axis_size("chan")
    spectra_total = spec_dev * tm_count
    raw_block = voltages.reshape(inp_dev, spec_dev, NFFT).transpose(1, 0, 2).astype(jnp.bfloat16)
    tail_block = shifted(raw_block[: TAPS - 1], "tm", -1)
    extended = jnp.concatenate([raw_block, tail_block], axis=0).astype(jnp.float32)
    coeffs = pfb_window()
    filtered = coeffs[0][None, None, :] * extended[0:spec_dev]
    for tap_index in range(1, TAPS):
        filtered = (
            filtered + coeffs[tap_index][None, None, :] * extended[tap_index : tap_index + spec_dev]
        )
    freq_re, freq_im = transform(filtered.reshape(spec_dev * inp_dev, FA, FB))
    packed = (jnp.stack([freq_re, freq_im]) * (1.0 / 64.0)).astype(jnp.bfloat16)
    packed = packed.reshape(2, CH, spec_dev, inp_dev)
    chan_local = CH // (tm_count * chan_count)
    reordered = packed.reshape(2, tm_count, chan_count, chan_local, spec_dev, inp_dev)
    reordered = reordered.transpose(0, 2, 1, 3, 4, 5).reshape(2, CH, spec_dev, inp_dev)
    sectioned = lax.all_to_all(reordered, "chan", split_axis=1, concat_axis=3, tiled=True)
    turned = lax.all_to_all(sectioned, "tm", split_axis=1, concat_axis=2, tiled=True)
    a_re = turned[0].astype(jnp.float32)
    a_im = turned[1].astype(jnp.float32)
    g_re = cal_gains[0][:, None, :]
    g_im = cal_gains[1][:, None, :]
    cal_re = (g_re * a_re - g_im * a_im).astype(jnp.bfloat16)
    cal_im = (g_re * a_im + g_im * a_re).astype(jnp.bfloat16)
    stacked = jnp.concatenate([cal_re, cal_im], axis=1)
    flipped = jnp.concatenate([cal_im, -cal_re], axis=1)
    vis_re = jnp.einsum("ctp,ctq->cpq", stacked, stacked, preferred_element_type=jnp.float32)
    vis_im = jnp.einsum("ctp,ctq->cpq", flipped, stacked, preferred_element_type=jnp.float32)
    visibilities = (jnp.stack([vis_re, vis_im]) / spectra_total).astype(jnp.bfloat16)
    chan_first = (
        lax.axis_index("tm") * (chan_local * chan_count) + lax.axis_index("chan") * chan_local
    )
    chan_ids = chan_first + jnp.arange(chan_local, dtype=jnp.int32)
    phase_idx = beam_delays[None, :, :] * chan_ids[:, None, None] % NFFT
    angles = phase_idx.astype(jnp.float32) * (2.0 * math.pi / NFFT)
    weight_norm = 1.0 / math.sqrt(beam_delays.shape[1])
    weight_re = (jnp.cos(angles) * weight_norm).astype(jnp.bfloat16)
    weight_im = (-jnp.sin(angles) * weight_norm).astype(jnp.bfloat16)
    beam_re = jnp.einsum(
        "cti,cbi->ctb", cal_re, weight_re, preferred_element_type=jnp.float32
    ) - jnp.einsum("cti,cbi->ctb", cal_im, weight_im, preferred_element_type=jnp.float32)
    beam_im = jnp.einsum(
        "cti,cbi->ctb", cal_im, weight_re, preferred_element_type=jnp.float32
    ) + jnp.einsum("cti,cbi->ctb", cal_re, weight_im, preferred_element_type=jnp.float32)
    beam_power = (beam_re * beam_re + beam_im * beam_im).astype(jnp.bfloat16)
    return (visibilities, beam_power)


def solution(mesh):
    return jax.shard_map(
        shards,
        mesh=mesh,
        in_specs=(P(("grp", "chan"), "tm"), P(), P(None, ("grp", "tm", "chan"), None)),
        out_specs=(
            P(None, ("grp", "tm", "chan"), None, None),
            P(("grp", "tm", "chan"), None, None),
        ),
        check_vma=False,
    )
```

profile of v0, /device:TPU:9, one launch (start us, length us, event | category | flops | bytes accessed | tf_op | source)
XLA Modules:
  0.0 799.1 jit_solution(1107052309619305802)
XLA Ops:
  0.6 2.4 convert_element_type.86
  3.0 0.2 copy.73
  3.2 1.3 slice.59
  4.5 1.9 collective-permute-start
  6.4 0.9 multiply_reduce_fusion
  8.0 0.1 fusion.81
  8.2 0.3 broadcast_divide_fusion
  8.5 33.4 %collective-permute-done = bf16[3,64,4096]{2,1,0:T(8,128)(2,1)} collective-permute-done((bf16[3,64,4096]{2,1,0:T(8,128)(2,1)}, bf16[3,64,4096]{2,1,0:T(8,128)(2,1)}, u32[]{:S(2)}, u32[]{:S(2)}) %collective-permute-start) | collective-permute-done | bytes 1572896 | tf_op jit(solution)/shard_map/ppermute | solution.py:18
  42.0 1.9 maximum_convert_fusion
  43.8 3.2 fusion.8
  47.1 7.8 reshape.80
  54.9 8.7 %copy.39 = f32[256,64,64]{0,1,2:T(8,128)} copy(f32[256,64,64]{2,1,0:T(8,128)} %reshape.80) | data formatting | bytes 8388608 | tf_op jit(solution)/shard_map/reshape | solution.py:74
  63.6 0.0 copy-start
  63.6 6.0 fusion.61
  69.6 0.0 copy-done
  69.6 6.0 add_bitcast_fusion
  75.6 4.6 fusion.12
  80.2 5.0 fusion.14
  85.2 6.0 add_bitcast_fusion.1
  91.2 4.7 subtract_bitcast_fusion.1
  96.0 4.7 copy.46
  100.7 3.6 stack.17
  104.3 5.6 copy.43
  109.8 4.9 stack.16
  114.7 3.3 fusion.20
  118.0 7.5 copy.55
  125.6 4.9 reshape.88
  130.5 29.5 %all_to_all.33 = bf16[4,2,131072]{2,1,0:T(2,128)(2,1)} all-to-all(bf16[4,2,131072]{2,1,0:T(2,128)(2,1)S(1)} %reshape.88), channel_id=1, replica_groups=mesh['grp'=2,'tm'=4,'chan'=4] {'chan'}, dimensions={0} | all-to-all | bytes 4194304 | tf_op jit(solution)/shard_map/all_to_all | solution.py:80
  160.0 5.8 reshape.89
  165.8 5.6 copy.50
  171.4 0.0 copy-start.3
  171.4 3.1 copy.51
  174.4 3.7 all-to-all-start.1
  178.2 0.0 copy-done.3
  178.2 43.9 %all-to-all-done.1 = bf16[2,512,4,256]{3,2,0,1:T(4,128)(2,1)S(1)} async-done(((bf16[2,512,4,256]{3,2,0,1:T(4,128)(2,1)}), bf16[2,512,4,256]{3,2,0,1:T(4,128)(2,1)S(1)}, u32[]{:S(2)}, u32[]{:S(2)}) %all-to-all-start.1) | async-done | bytes 2097184 | tf_op jit(solution)/shard_map/all_to_all | solution.py:81
  222.1 0.4 copy.52
  222.5 1.7 slice_convert_fusion.1
  224.2 2.7 copy.53
  226.9 2.0 reshape.82
  228.9 4.3 copy.54
  233.2 2.9 reshape.83
  236.1 0.0 copy-start.1
  236.1 2.3 add_convert_fusion.1
  238.5 0.0 copy-done.1
  238.5 0.0 copy-start.4
  238.5 1.7 fusion.140
  240.1 0.0 copy-done.4
  240.1 125.3 %fusion.6 = f32[128,16,256]{2,1,0:T(8,128)} fusion(bf16[128,16,256]{2,1,0:T(8,128)(2,1)S(1)} %get-tuple-element.3, s32[128]{0:T(128)S(1)} %iota_add_fusion.2, s32[256,256]{1,0:T(8,128)S(1)} %copy-done.4), kind=kOutput, calls=%fused_computation.14 | convolution fusion | flops 411041792 | bytes 3408384 | tf_op jit(solution)/shard_map/cti,cbi->ctb/dot_general | solution.py:107
  365.4 123.7 %fusion.5 = f32[128,16,256]{2,1,0:T(8,128)} fusion(bf16[128,16,256]{2,1,0:T(8,128)(2,1)S(1)} %get-tuple-element.3, s32[128]{0:T(128)S(1)} %iota_add_fusion.2, s32[256,256]{1,0:T(8,128)S(1)} %copy-done.4), kind=kOutput, calls=%fused_computation.13 | convolution fusion | flops 402653184 | bytes 3408384 | tf_op jit(solution)/shard_map/cti,cbi->ctb/dot_general | solution.py:102
  489.2 124.2 %fusion.4 = f32[128,16,256]{2,1,0:T(8,128)} fusion(bf16[128,16,256]{2,1,0:T(8,128)(2,1)S(1)} %add_convert_fusion.1, s32[128]{0:T(128)S(1)} %iota_add_fusion.2, s32[256,256]{1,0:T(8,128)S(1)} %copy-done.4), kind=kOutput, calls=%fused_computation.12 | convolution fusion | flops 402653184 | bytes 3408384 | tf_op jit(solution)/shard_map/cti,cbi->ctb/dot_general | solution.py:105
  613.4 0.0 copy-start.2
  613.4 13.1 %convolution_bitcast_fusion.1 = f32[1,128,256,256]{3,2,1,0:T(8,128)} fusion(bf16[128,16,256]{2,1,0:T(8,128)(2,1)S(1)} %add_convert_fusion.1, bf16[128,16,256]{2,1,0:T(8,128)(2,1)S(1)} %get-tuple-element.3), kind=kOutput, calls=%fused_computation.17 | convolution fusion | flops 541065216 | bytes 35651584 | tf_op jit(solution)/shard_map/ctp,ctq->cpq/dot_general | solution.py:90
  626.5 0.0 copy-done.2
  626.5 13.1 %convolution_bitcast_fusion = f32[1,128,256,256]{3,2,1,0:T(8,128)} fusion(bf16[128,16,256]{2,1,0:T(8,128)(2,1)S(1)} %copy-done.2, bf16[128,16,256]{2,1,0:T(8,128)(2,1)S(1)} %add_convert_fusion.1, bf16[128,16,256]{2,1,0:T(8,128)(2,1)S(1)} %get-tuple-element.3), kind=kOutput, calls=%fused_computation.16 | convolution fusion | flops 545259520 | bytes 36700160 | tf_op jit(solution)/shard_map/ctp,ctq->cpq/dot_general | solution.py:91
  639.7 0.0 copy-start.5
  639.7 32.8 %fusion = bf16[2,128,256,256]{3,2,1,0:T(8,128)(2,1)} fusion(f32[1,128,256,256]{3,2,1,0:T(8,128)} %convolution_bitcast_fusion, f32[1,128,256,256]{3,2,1,0:T(8,128)} %convolution_bitcast_fusion.1), kind=kLoop, calls=%fused_computation.1 | loop fusion | flops 50331648 | bytes 100663296 | tf_op jit(solution)/shard_map/convert_element_type | solution.py:92
  672.4 0.0 copy-done.5
  672.4 126.5 %add_convert_fusion = bf16[128,16,256]{2,1,0:T(8,128)(2,1)} fusion(f32[128,16,256]{2,1,0:T(8,128)} %fusion.4, f32[128,16,256]{2,1,0:T(8,128)} %fusion.6, f32[128,16,256]{2,1,0:T(8,128)} %fusion.5, bf16[128,16,256]{2,1,0:T(8,128)(2,1)S(1)} %add_convert_fusion.1, s32[128]{0:T(128)S(1)} %iota_add_fusion.2, s32[256,256]{1,0:T(8,128)S(1)} %copy-done.5), kind=kOutput, calls=%fused_computation.44 | convolution fusion | flops 414187520 | bytes 8651264 | tf_op jit(solution)/shard_map/cti,cbi->ctb/dot_general | solution.py:104
  (3 shorter events, 0.0 us)
Async XLA Ops:
  4.5 37.5 %collective-permute-start = (bf16[3,64,4096]{2,1,0:T(8,128)(2,1)}, bf16[3,64,4096]{2,1,0:T(8,128)(2,1)}, u32[]{:S(2)}, u32[]{:S(2)}) collective-permute-start(bf16[3,64,4096]{2,1,0:T(8,128)(2,1)} %slice.59), channel_id=1, source_target_pairs={{4,0},{8,4},{12,8},{5,1},{9,5},{13,9},{6,2},{10,6},{14,10},{7,3},{... | collective-permute-start | bytes 4718600 | tf_op jit(solution)/shard_map/ppermute | solution.py:18
  63.6 6.1 copy-start
  171.4 6.8 copy-start.3
  174.4 47.7 %all-to-all-start.1 = ((bf16[2,512,4,256]{3,2,0,1:T(4,128)(2,1)}), bf16[2,512,4,256]{3,2,0,1:T(4,128)(2,1)S(1)}, u32[]{:S(2)}, u32[]{:S(2)}) async-start(bf16[2,512,4,256]{3,2,0,1:T(4,128)(2,1)} %copy.51), calls=%async_computation.1 | async-start | bytes 4194304 | tf_op jit(solution)/shard_map/all_to_all | solution.py:81
  236.1 2.3 copy-start.1
  238.5 1.7 copy-start.4
  613.4 13.2 %copy-start.2 = (bf16[128,16,256]{2,1,0:T(8,128)(2,1)S(1)}, bf16[128,16,256]{2,1,0:T(8,128)(2,1)}, u32[]{:S(2)}) copy-start(bf16[128,16,256]{2,1,0:T(8,128)(2,1)} %get-tuple-element.2) | copy-start | bytes 3145732
  639.7 32.8 %copy-start.5 = (s32[256,256]{1,0:T(8,128)S(1)}, s32[256,256]{1,0:T(8,128)}, u32[]{:S(2)}) copy-start(s32[256,256]{1,0:T(8,128)} %param.4) | copy-start | bytes 786436
where the time goes:
time: 812 us; the launch traced here: 799 us
  matrix products  558 us (69%)
  waiting for transfers between devices  77.3 us (10%)
  local copies, waits for them, and re-layouts  75.9 us (9%)
  other arithmetic  50.7 us (6%)
  blocking collectives  29.5 us (4%)
    dot_general x1, matrix products, shards(): jnp.einsum('cti,cbi->ctb', cal_im, weight_im, preferred_element_type=jnp....  126 us
    dot_general x1, matrix products, shards(): jnp.einsum('cti,cbi->ctb', cal_re, weight_im, preferred_element_type=jnp....  125 us
    dot_general x1, matrix products, shards(): jnp.einsum('cti,cbi->ctb', cal_im, weight_re, preferred_element_type=jnp....  124 us
    dot_general x1, matrix products, shards(): jnp.einsum('cti,cbi->ctb', cal_re, weight_re, preferred_element_type=jnp....  124 us
    all_to_all x1, waiting for transfers between devices, shards(): lax.all_to_all(sectioned, 'tm', split_axis=1, concat_axis=2, tiled=True)  43.9 us
    ppermute x1, waiting for transfers between devices, shifted(): return lax.ppermute(block, axis, route)  33.4 us
    convert_element_type x1, other arithmetic, shards(): (jnp.stack([vis_re, vis_im]) / spectra_total).astype(jnp.bfloat16)  32.8 us
    all_to_all x1, blocking collectives, shards(): lax.all_to_all(reordered, 'chan', split_axis=1, concat_axis=3, tiled=True)  29.5 us
  transfers between devices with their start and end apart: 2, of which 2 were waited for; matrix products, arithmetic and copies ran while one was open for 0% of the time, Pallas kernels for 0%

commit v1 on v0

--- a/solution.py
+++ b/solution.py
@@ -1,8 +1,12 @@
+import functools
 import math
 
 import jax
 import jax.numpy as jnp
+import numpy as np
 from jax import lax
+from jax.experimental import pallas as pl
+from jax.experimental.pallas import tpu as pltpu
 from jax.sharding import PartitionSpec as P
 
 TAPS = 4
@@ -10,12 +14,326 @@
 FB = 64
 NFFT = 4096
 CH = 2048
+RAD = 32
+LANES = 128
+PAIRS = RAD // 2
+ROWS = NFFT // PAIRS
+CHAN_BLOCK = 8
+ROT = 16
+MIB = 1 << 20
 
 
 def shifted(block, axis, distance):
     devices = range(lax.axis_size(axis))
     route = [(i - distance, i) for i in devices if i - distance in devices]
     return lax.ppermute(block, axis, route)
+
+
+def window_table():
+    total_len = TAPS * NFFT
+    pos = np.arange(total_len, dtype=np.float64)
+    centre = (pos - total_len / 2 + 0.5) / NFFT
+    taper = 0.5 - 0.5 * np.cos(2.0 * np.pi * (pos + 0.5) / total_len)
+    coeffs = np.sinc(centre) * taper
+    coeffs = coeffs / np.sqrt(np.sum(coeffs * coeffs))
+    return coeffs.reshape(TAPS, NFFT).astype(np.float32)
+
+
+def split_table(table):
+    high = table.astype(jnp.bfloat16)
+    low = (table - high.astype(np.float64)).astype(jnp.bfloat16)
+    return high, low
+
+
+def second_tables():
+    lane = np.arange(LANES)
+    k1 = np.arange(CH // RAD)
+    table = np.zeros((PAIRS, CH // RAD, 2, 2, 2, LANES))
+    for m in range(PAIRS):
+        if m == 0:
+            for which, k2 in enumerate((0, RAD // 2)):
+                phase = (RAD * k1[:, None] + k2) * lane[None, :] % NFFT
+                angle = 2.0 * np.pi * phase / NFFT
+                table[m, :, which, 0, which] = np.cos(angle)
+                table[m, :, which, 1, which] = -np.sin(angle)
+            continue
+        for which in range(2):
+            channel = RAD * k1 + (m if which == 0 else RAD - m)
+            source = channel if which == 0 else NFFT - channel
+            sign = 1.0 if which == 0 else -1.0
+            angle = 2.0 * np.pi * (source[:, None] * lane[None, :] % NFFT) / NFFT
+            cos, sin = np.cos(angle), np.sin(angle)
+            table[m, :, which, 0, 0] = cos
+            table[m, :, which, 0, 1] = sin
+            table[m, :, which, 1, 0] = -sin * sign
+            table[m, :, which, 1, 1] = cos * sign
+    return split_table(table.reshape(PAIRS, ROWS, 2 * LANES) / 64.0)
+
+
+def real_transform(vals):
+    n = len(vals)
+    if n == 2:
+        return [(vals[0] + vals[1], None), (vals[0] - vals[1], None)]
+    even = real_transform(vals[0::2])
+    odd = real_transform(vals[1::2])
+    half = n // 2
+    out = [None] * (half + 1)
+    out[0] = (even[0][0] + odd[0][0], None)
+    out[half] = (even[0][0] - odd[0][0], None)
+    for k in range(1, n // 4):
+        c, s = math.cos(2 * math.pi * k / n), math.sin(2 * math.pi * k / n)
+        (er, ei), (sr, si) = even[k], odd[k]
+        if 8 * k == n:
+            tr, ti = (sr + si) * c, (si - sr) * c
+        else:
+            tr, ti = sr * c + si * s, si * c - sr * s
+        out[k] = (er + tr, ei + ti)
+        out[half - k] = (er - tr, ti - ei)
+    out[n // 4] = (even[n // 4][0], -odd[n // 4][0])
+    return out
+
+
+def spectra_kernel(spec, rows_in, steps_in, pairs, x_ref, halo_ref, win_ref, high_ref, low_ref, out_ref, wide, mid):
+    step = pl.program_id(0)
+
+    @pl.when(step < steps_in)
+    def _():
+        own = spec * NFFT
+        wide[:, :own] = x_ref[...].astype(jnp.float32)
+        wide[:, own:] = halo_ref[...].astype(jnp.float32)
+        inputs = rows_in * steps_in
+
+        @pl.loop(0, rows_in // 8)
+        def _(sub):
+            rows = pl.ds(pl.multiple_of(sub * 8, 8), 8)
+            for s in range(spec):
+                vals = []
+                for col in range(RAD):
+                    total = None
+                    for tap in range(TAPS):
+                        at = (s + tap) * NFFT + col * LANES
+                        term = wide[rows, at : at + LANES] * win_ref[tap : tap + 1, col * LANES : (col + 1) * LANES]
+                        total = term if total is None else total + term
+                    vals.append(total)
+                freq = real_transform(vals)
+                place = pl.ds(pl.multiple_of(s * inputs + step * rows_in + sub * 8, 8), 8)
+                mid[0, place, :LANES] = freq[0][0]
+                mid[0, place, LANES:] = freq[PAIRS][0]
+                for m in range(1, PAIRS):
+                    mid[m, place, :LANES] = freq[m][0]
+                    mid[m, place, LANES:] = freq[m][1]
+
+    @pl.when(step >= steps_in)
+    def _():
+        first = (step - steps_in) * pairs
+        owners, _, lanes = out_ref.shape
+        per = ROWS // owners
+        for p in range(pairs):
+            both = mid[first + p]
+            high = both.astype(jnp.bfloat16)
+            low = (both - high.astype(jnp.float32)).astype(jnp.bfloat16)
+            left = jnp.concatenate([high_ref[p], high_ref[p], low_ref[p]], axis=1)
+            right = jnp.concatenate([high, low, high], axis=1)
+            total = lax.dot_general(left, right, (((1,), (1,)), ((), ())), preferred_element_type=jnp.float32)
+            out_ref[:, p * per : (p + 1) * per, :] = total.reshape(owners, per, lanes).astype(jnp.bfloat16)
+
+
+def spectra(voltages, halo, owners):
+    inputs = voltages.shape[0]
+    spec = voltages.shape[1] // NFFT
+    lanes = inputs * spec
+    rows_in, pairs = 16, 4
+    steps_in, steps_out = inputs // rows_in, PAIRS // pairs
+    per = ROWS // owners
+    high, low = second_tables()
+    before = lambda g: jnp.minimum(g, steps_in - 1)
+    after = lambda g: jnp.maximum(g - steps_in, 0)
+    return pl.pallas_call(
+        functools.partial(spectra_kernel, spec, rows_in, steps_in, pairs),
+        grid=(steps_in + steps_out,),
+        in_specs=[
+            pl.BlockSpec((rows_in, spec * NFFT), lambda g: (before(g), 0)),
+            pl.BlockSpec((rows_in, (TAPS - 1) * NFFT), lambda g: (before(g), 0)),
+            pl.BlockSpec((TAPS, NFFT), lambda g: (0, 0)),
+            pl.BlockSpec((pairs, ROWS, 2 * LANES), lambda g: (after(g), 0, 0)),
+            pl.BlockSpec((pairs, ROWS, 2 * LANES), lambda g: (after(g), 0, 0)),
+        ],
+        out_specs=pl.BlockSpec((owners, pairs * per, lanes), lambda g: (0, after(g), 0)),
+        out_shape=jax.ShapeDtypeStruct((owners, PAIRS * per, lanes), jnp.bfloat16),
+        scratch_shapes=[
+            pltpu.VMEM((rows_in, (spec + TAPS - 1) * NFFT), jnp.float32),
+            pltpu.VMEM((PAIRS, lanes, 2 * LANES), jnp.float32),
+        ],
+        compiler_params=pltpu.CompilerParams(vmem_limit_bytes=40 * MIB),
+        cost_estimate=pl.CostEstimate(flops=6 * PAIRS * ROWS * 256 * lanes, bytes_accessed=12 * MIB, transcendentals=0),
+        name="spectra",
+    )(voltages, halo, jnp.asarray(window_table()), jnp.asarray(high), jnp.asarray(low))
+
+
+def unit_circle(phase):
+    quarter = NFFT // 4
+    quad = (phase + quarter // 2) // quarter
+    x = (phase - quad * quarter).astype(jnp.float32) * (2.0 * math.pi / NFFT)
+    q = x * x
+    cos = 1.0 + q * (-1 / 2 + q * (1 / 24 + q * (-1 / 720 + q * (1 / 40320))))
+    sin = x * (1.0 + q * (-1 / 6 + q * (1 / 120 + q * (-1 / 5040 + q * (1 / 362880)))))
+    odd = quad % 2 == 1
+    c, s = jnp.where(odd, sin, cos), jnp.where(odd, cos, sin)
+    c = jnp.where((quad == 1) | (quad == 2), -c, c)
+    s = jnp.where((quad == 2) | (quad == 3), -s, s)
+    return c, s
+
+
+def weights_kernel(norm, first_ref, delay_ref, out_ref):
+    delays = delay_ref[...]
+    step_cos, step_sin = unit_circle(delays)
+
+    @pl.loop(0, out_ref.shape[0] // ROT)
+    def _(group):
+        c, s = unit_circle(delays * (first_ref[0] + group * ROT) % NFFT)
+        c, s = c * norm, s * -norm
+        for j in range(ROT):
+            k = group * ROT + j
+            out_ref[k, 0] = c.astype(jnp.bfloat16)
+            out_ref[k, 1] = s.astype(jnp.bfloat16)
+            if j + 1 < ROT:
+                c, s = c * step_cos + s * step_sin, s * step_cos - c * step_sin
+
+
+def beam_weights(beam_delays, chan_first, chan_local):
+    beams, inputs = beam_delays.shape
+    rows = 16
+    return pl.pallas_call(
+        functools.partial(weights_kernel, 1.0 / math.sqrt(inputs)),
+        grid=(inputs // rows,),
+        in_specs=[
+            pl.BlockSpec(memory_space=pltpu.SMEM),
+            pl.BlockSpec((rows, beams), lambda g: (g, 0)),
+        ],
+        out_specs=pl.BlockSpec((chan_local, 2, rows, beams), lambda g: (0, 0, g, 0)),
+        out_shape=jax.ShapeDtypeStruct((chan_local, 2, inputs, beams), jnp.bfloat16),
+        compiler_params=pltpu.CompilerParams(vmem_limit_bytes=24 * MIB),
+        cost_estimate=pl.CostEstimate(
+            flops=60 * chan_local * inputs * beams, bytes_accessed=4 * chan_local * inputs * beams, transcendentals=0
+        ),
+        name="weights",
+    )(chan_first.reshape(1), beam_delays.T)
+
+
+def combine_kernel(tm_count, spec, inputs, g_ref, gain_ref, w_ref, vis_ref, power_ref, rows_ref):
+    step = pl.program_id(0)
+    rows = g_ref.shape[1]
+    per = rows // PAIRS
+    times = tm_count * spec
+    half = LANES // 2
+
+    @pl.when(step == 0)
+    def _():
+        low_half = lax.broadcasted_iota(jnp.int32, (per, LANES), 1) < half
+
+        @pl.loop(0, PAIRS)
+        def _(m):
+            at = pl.ds(pl.multiple_of(m * per, per), per)
+            for t in range(tm_count):
+                for pair in range(2):
+                    for two in range(2):
+                        cols = slice(two * LANES, (two + 1) * LANES)
+                        a = g_ref[t * 4 + 2 * pair, at, cols].astype(jnp.float32)
+                        b = g_ref[t * 4 + 2 * pair + 1, at, cols].astype(jnp.float32)
+                        even = jnp.where(low_half, a, pltpu.roll(b, half, 1))
+                        odd = jnp.where(low_half, pltpu.roll(a, half, 1), b)
+                        s = t * spec + 2 * two
+                        rows_ref[pair, pl.ds(pl.multiple_of(s * rows + m * per, per), per), :] = even
+                        rows_ref[pair, pl.ds(pl.multiple_of((s + 1) * rows + m * per, per), per), :] = odd
+
+    scale = 1.0 / times
+    blocks = RAD // CHAN_BLOCK
+    for u in range(CHAN_BLOCK):
+        k = step * CHAN_BLOCK + u
+        k2 = (step % blocks) * CHAN_BLOCK + u
+        upper = k2 // PAIRS
+        m = jnp.where(k2 == PAIRS, 0, jnp.where(upper == 1, RAD - k2, k2))
+        row = m * per + (step // blocks) * 4 + upper * 2
+        z_re = jnp.concatenate([rows_ref[p, pl.ds(row, times, stride=rows), :] for p in range(2)], axis=1)
+        z_im = jnp.concatenate([rows_ref[p, pl.ds(row + 1, times, stride=rows), :] for p in range(2)], axis=1)
+        g_re = gain_ref[0, u : u + 1, :]
+        g_im = gain_ref[1, u : u + 1, :]
+        cal_re = (g_re * z_re - g_im * z_im).astype(jnp.bfloat16)
+        cal_im = (g_re * z_im + g_im * z_re).astype(jnp.bfloat16)
+        stacked = jnp.concatenate([cal_re, cal_im], axis=0)
+        turned = jnp.concatenate([-cal_im, cal_re], axis=0)
+        both = jnp.concatenate([stacked, turned], axis=1)
+        vis = lax.dot_general(stacked, both, (((0,), (0,)), ((), ())), preferred_element_type=jnp.float32)
+        vis = (vis * scale).astype(jnp.bfloat16)
+        vis_ref[0, u] = vis[:, :inputs]
+        vis_ref[1, u] = vis[:, inputs:]
+        left = jnp.concatenate([stacked, turned], axis=1)
+        w = w_ref[u].reshape(2 * inputs, w_ref.shape[3])
+        formed = lax.dot_general(left, w, (((1,), (0,)), ((), ())), preferred_element_type=jnp.float32)
+        formed = formed * formed
+        power_ref[u] = (formed[:times] + formed[times:]).astype(jnp.bfloat16)
+
+
+def combine(gathered, cal_gains, weights, tm_count, spec):
+    sources, rows, lanes = gathered.shape
+    chan_local, _, inputs, beams = weights.shape
+    times = tm_count * spec
+    return pl.pallas_call(
+        functools.partial(combine_kernel, tm_count, spec, inputs),
+        grid=(chan_local // CHAN_BLOCK,),
+        in_specs=[
+            pl.BlockSpec((sources, rows, lanes), lambda g: (0, 0, 0)),
+            pl.BlockSpec((2, CHAN_BLOCK, inputs), lambda g: (0, g, 0)),
+            pl.BlockSpec((CHAN_BLOCK, 2, inputs, beams), lambda g: (g, 0, 0, 0)),
+        ],
+        out_specs=[
+            pl.BlockSpec((2, CHAN_BLOCK, inputs, inputs), lambda g: (0, g, 0, 0)),
+            pl.BlockSpec((CHAN_BLOCK, times, beams), lambda g: (g, 0, 0)),
+        ],
+        out_shape=[
+            jax.ShapeDtypeStruct((2, chan_local, inputs, inputs), jnp.bfloat16),
+            jax.ShapeDtypeStruct((chan_local, times, beams), jnp.bfloat16),
+        ],
+        scratch_shapes=[pltpu.VMEM((2, times * rows, LANES), jnp.float32)],
+        compiler_params=pltpu.CompilerParams(vmem_limit_bytes=40 * MIB),
+        cost_estimate=pl.CostEstimate(
+            flops=chan_local * (4 * 2 * times * inputs * inputs + 8 * times * inputs * beams),
+            bytes_accessed=chan_local * (4 * inputs * inputs + 4 * inputs * beams),
+            transcendentals=0,
+        ),
+        name="combine",
+    )(gathered, cal_gains, weights)
+
+
+def fits(voltages, beam_delays, tm_count, chan_count):
+    inp_dev, samples = voltages.shape
+    spec = samples // NFFT
+    owners = tm_count * chan_count
+    return (
+        ROWS % owners == 0
+        and ROWS // owners == 16
+        and spec == 4
+        and chan_count == 4
+        and inp_dev * 2 == LANES
+        and beam_delays.shape[1] == inp_dev * chan_count
+    )
+
+
+def shards(voltages, beam_delays, cal_gains):
+    tm_count = lax.axis_size("tm")
+    chan_count = lax.axis_size("chan")
+    if not fits(voltages, beam_delays, tm_count, chan_count):
+        return plain_shards(voltages, beam_delays, cal_gains)
+    owners = tm_count * chan_count
+    chan_local = CH // owners
+    spec_dev = voltages.shape[1] // NFFT
+    halo = shifted(voltages[:, : (TAPS - 1) * NFFT].astype(jnp.bfloat16), "tm", -1)
+    chan_first = (lax.axis_index("tm") * chan_count + lax.axis_index("chan")) * chan_local
+    weights = beam_weights(beam_delays, chan_first, chan_local)
+    sent = spectra(voltages, halo, owners)
+    gathered = lax.all_to_all(sent, ("tm", "chan"), split_axis=0, concat_axis=0, tiled=True)
+    visibilities, beam_power = combine(gathered, cal_gains, weights, tm_count, spec_dev)
+    return (visibilities, beam_power)
 
 
 def pfb_window():
@@ -56,7 +374,7 @@
     return (freq_re.reshape(CH, row_count), freq_im.reshape(CH, row_count))
 
 
-def shards(voltages, beam_delays, cal_gains):
+def plain_shards(voltages, beam_delays, cal_gains):
     inp_dev = voltages.shape[0]
     spec_dev = voltages.shape[1] // NFFT
     tm_count = lax.axis_size("tm")

time: 812 us -> 140 us (0.17); the launches traced: 799 us -> 138 us
  matrix products: 558 us -> 0 us
  local copies, waits for them, and re-layouts: 75.9 us -> 4.65 us
  Pallas kernels: 0 us -> 59.7 us
  other arithmetic: 50.7 us -> 2.2 us
  blocking collectives: 29.5 us -> 0 us
  waiting for transfers between devices: 77.3 us -> 62.3 us
    dot_general x12 -> x0, matrix products: 558 us -> none  [the longest x1 126 us: shards(): jnp.einsum('cti,cbi->ctb', cal_im, weight_im, preferred_element_type=jnp....]
    pallas_call x0 -> x3, Pallas kernels: none -> 59.7 us  [the longest x1 35.4 us: combine(): pl.pallas_call(functools.partial(combine_kernel, tm_count, spec, inputs),...]
    convert_element_type x5 -> x0, other arithmetic: 41.1 us -> none  [the longest x1 32.8 us: shards(): (jnp.stack([vis_re, vis_im]) / spectra_total).astype(jnp.bfloat16)]
    all_to_all x1 -> x0, blocking collectives: 29.5 us -> none  [shards(): lax.all_to_all(reordered, 'chan', split_axis=1, concat_axis=3, tiled=True)]
    reshape x3 -> x0, local copies, waits for them, and re-layouts: 24 us -> none  [the longest x2 16.5 us: shards(): freq_re, freq_im = transform(filtered.reshape(spec_dev * inp_dev, FA, FB))]
    all_to_all x1, waiting for transfers between devices: 43.9 us -> 27.1 us  [shards(): lax.all_to_all(sent, ('tm', 'chan'), split_axis=0, concat_axis=0, tiled=T...]
    convert_element_type x5 -> x0, local copies, waits for them, and re-layouts: 12.1 us -> none  [the longest x2 7.2 us: shards(): a_im = turned[1].astype(jnp.float32)]
    all_to_all x3 -> x0, local copies, waits for them, and re-layouts: 9.07 us -> none  [the longest x2 8.65 us: shards(): lax.all_to_all(reordered, 'chan', split_axis=1, concat_axis=3, tiled=True)]
  transfers between devices with their start and end apart: 2 -> 2, of which waited for: 2 -> 2; matrix products, arithmetic and copies ran while one was open for 0% -> 0% of each run, Pallas kernels for 0% -> 14%
where the time goes in v1:
time: 140 us; the launch traced here: 138 us
  waiting for transfers between devices  62.3 us (44%)
  Pallas kernels  59.7 us (43%)
  starting transfers between devices  8.62 us (6%)
  local copies, waits for them, and re-layouts  4.65 us (3%)
  other arithmetic  2.2 us (2%)
    pallas_call x1, Pallas kernels, combine(): pl.pallas_call(functools.partial(combine_kernel, tm_count, spec, inputs),...  35.4 us
    ppermute x1, waiting for transfers between devices, shifted(): return lax.ppermute(block, axis, route)  35.2 us
    all_to_all x1, waiting for transfers between devices, shards(): lax.all_to_all(sent, ('tm', 'chan'), split_axis=0, concat_axis=0, tiled=T...  27.1 us
    pallas_call x1, Pallas kernels, beam_weights(): pl.pallas_call(functools.partial(weights_kernel, 1.0 / math.sqrt(inputs))...  18.7 us
    all_to_all x1, starting transfers between devices, shards(): lax.all_to_all(sent, ('tm', 'chan'), split_axis=0, concat_axis=0, tiled=T...  6.57 us
    pallas_call x1, Pallas kernels, spectra(): pl.pallas_call(functools.partial(spectra_kernel, spec, rows_in, steps_in,...  5.55 us
    unnamed x15, local copies, waits for them, and re-layouts  4.65 us
  transfers between devices with their start and end apart: 2, of which 2 were waited for; matrix products, arithmetic and copies ran while one was open for 0% of the time, Pallas kernels for 14%

profile of v1, /device:TPU:9, one launch (start us, length us, event | category | flops | bytes accessed | tf_op | source)
XLA Modules:
  0.0 138.2 jit_solution(12172591938944169204)
XLA Ops:
  0.6 0.0 copy-start.5
  0.6 0.0 copy-start
  0.7 2.2 %slice_convert_fusion = bf16[64,12288]{1,0:T(8,128)(2,1)S(1)} fusion(s32[64,16384]{1,0:T(8,128)} %x_ref.1), kind=kLoop, calls=%fused_computation | loop fusion | flops 786432 | bytes 4718592 | tf_op jit(solution)/shard_map/convert
  2.9 2.1 %collective-permute-start = (bf16[64,12288]{1,0:T(8,128)(2,1)S(1)}, bf16[64,12288]{1,0:T(8,128)(2,1)S(1)}, u32[]{:S(2)}, u32[]{:S(2)}) collective-permute-start(bf16[64,12288]{1,0:T(8,128)(2,1)S(1)} %slice_convert_fusion), channel_id=1, source_target_pairs={{4,0},{8,4},{12,8},{5,1},{9,5},{13,9},{6,2},{10,6},{14,10},{7,3},{... | collective-permute-start | bytes 4718600 | tf_op jit(solution)/shard_map/ppermute | solution.py:29
  4.9 35.2 %collective-permute-done.halo_ref = bf16[64,12288]{1,0:T(8,128)(2,1)S(1)} collective-permute-done((bf16[64,12288]{1,0:T(8,128)(2,1)S(1)}, bf16[64,12288]{1,0:T(8,128)(2,1)S(1)}, u32[]{:S(2)}, u32[]{:S(2)}) %collective-permute-start) | collective-permute-done | bytes 1572896 | tf_op jit(solution)/shard_map/ppermute | solution.py:29
  40.1 0.0 copy-done.5
  40.1 0.0 copy-done
  40.1 0.0 copy-start.2
  40.1 1.6 %copy-done.2 = bf16[16,256,256]{2,1,0:T(8,128)(2,1)S(1)} copy-done((bf16[16,256,256]{2,1,0:T(8,128)(2,1)S(1)}, bf16[16,256,256]{2,1,0:T(8,128)(2,1)}, u32[]{:S(2)}) %copy-start.2) | copy-done | bytes 2097176
  41.7 0.0 copy-start.3
  41.7 1.6 %copy-done.3 = bf16[16,256,256]{2,1,0:T(8,128)(2,1)S(1)} copy-done((bf16[16,256,256]{2,1,0:T(8,128)(2,1)S(1)}, bf16[16,256,256]{2,1,0:T(8,128)(2,1)}, u32[]{:S(2)}) %copy-start.3) | copy-done | bytes 2097176
  43.3 5.5 %spectra.1 = bf16[16,256,256]{2,1,0:T(8,128)(2,1)S(1)} custom-call(s32[64,16384]{1,0:T(8,128)S(1)} %copy-done, bf16[64,12288]{1,0:T(8,128)(2,1)S(1)} %collective-permute-done.halo_ref, f32[4,4096]{1,0:T(4,128)S(1)} %copy-done.5, bf16[16,256,256]{2,1,0:T(8,128)(2,1)S(1)} %copy-done.3, bf16[16,256,256]{2,1,0:T(8,128)(2,1)S(1)} %copy-done.2), custom_call_target="tpu_custom_call" | custom-call | flops 1610612736 | bytes 12582912 | tf_op jit(solution)/shard_map/spectra/pallas_call | solution.py:151
  48.9 0.0 copy-start.1
  48.9 1.3 copy-done.1
  50.2 0.0 copy-start.6
  50.2 6.6 %all-to-all-start = ((bf16[16,256,256]{2,1,0:T(8,128)(2,1)}), bf16[16,256,256]{2,1,0:T(8,128)(2,1)S(1)}, u32[]{:S(2)}, u32[]{:S(2)}) async-start(bf16[16,256,256]{2,1,0:T(8,128)(2,1)} %copy-done.1), calls=%async_computation | async-start | bytes 4194304 | tf_op jit(solution)/shard_map/all_to_all | solution.py:334
  56.8 0.0 copy-done.6
  56.8 0.1 copy.8
  56.9 0.0 copy-start.4
  56.9 18.7 %weights.1.w_ref = bf16[128,2,256,256]{3,2,1,0:T(8,128)(2,1)} custom-call(s32[1]{0:T(128)} %bitcast.first_ref, s32[256,256]{1,0:T(8,128)S(1)} %bitcast.2), custom_call_target="tpu_custom_call" | custom-call | flops 503316480 | bytes 33554432 | tf_op jit(solution)/shard_map/weights/pallas_call | solution.py:206
  75.7 27.1 %all-to-all-done.g_ref = bf16[16,256,256]{2,1,0:T(8,128)(2,1)S(1)} async-done(((bf16[16,256,256]{2,1,0:T(8,128)(2,1)}), bf16[16,256,256]{2,1,0:T(8,128)(2,1)S(1)}, u32[]{:S(2)}, u32[]{:S(2)}) %all-to-all-start) | async-done | bytes 2097184 | tf_op jit(solution)/shard_map/all_to_all | solution.py:334
  102.8 0.0 copy-done.4
  102.8 35.4 %combine.1 = (bf16[2,128,256,256]{3,2,1,0:T(8,128)(2,1)}, bf16[128,16,256]{2,1,0:T(8,128)(2,1)}) custom-call(bf16[16,256,256]{2,1,0:T(8,128)(2,1)S(1)} %all-to-all-done.g_ref, f32[2,128,256]{2,1,0:T(8,128)S(1)} %copy-done.4, bf16[128,2,256,256]{3,2,1,0:T(8,128)(2,1)} %weights.1.w_ref), custom_call_target="tpu_custom_call" | custom-call | flops 2147483648 | bytes 67108864 | tf_op jit(solution)/shard_map/combine/pallas_call | solution.py:281
Async XLA Ops:
  0.6 39.5 %copy-start.5 = (f32[4,4096]{1,0:T(4,128)S(1)}, f32[4,4096]{1,0:T(4,128)}, u32[]{:S(2)}) copy-start(f32[4,4096]{1,0:T(4,128)} %constant.17.clone.win_ref) | copy-start | bytes 196612
  0.6 39.5 %copy-start = (s32[64,16384]{1,0:T(8,128)S(1)}, s32[64,16384]{1,0:T(8,128)}, u32[]{:S(2)}) copy-start(s32[64,16384]{1,0:T(8,128)} %x_ref.1) | copy-start | bytes 12582916
  2.9 37.3 %collective-permute-start = (bf16[64,12288]{1,0:T(8,128)(2,1)S(1)}, bf16[64,12288]{1,0:T(8,128)(2,1)S(1)}, u32[]{:S(2)}, u32[]{:S(2)}) collective-permute-start(bf16[64,12288]{1,0:T(8,128)(2,1)S(1)} %slice_convert_fusion), channel_id=1, source_target_pairs={{4,0},{8,4},{12,8},{5,1},{9,5},{13,9},{6,2},{10,6},{14,10},{7,3},{... | collective-permute-start | bytes 4718600 | tf_op jit(solution)/shard_map/ppermute | solution.py:29
  40.1 1.6 %copy-start.2 = (bf16[16,256,256]{2,1,0:T(8,128)(2,1)S(1)}, bf16[16,256,256]{2,1,0:T(8,128)(2,1)}, u32[]{:S(2)}) copy-start(bf16[16,256,256]{2,1,0:T(8,128)(2,1)} %constant.19.clone.low_ref) | copy-start | bytes 6291460
  41.7 1.6 %copy-start.3 = (bf16[16,256,256]{2,1,0:T(8,128)(2,1)S(1)}, bf16[16,256,256]{2,1,0:T(8,128)(2,1)}, u32[]{:S(2)}) copy-start(bf16[16,256,256]{2,1,0:T(8,128)(2,1)} %constant.18.clone.high_ref) | copy-start | bytes 6291460
  48.9 1.3 copy-start.1
  50.2 6.6 %copy-start.6 = (s32[256,256]{1,0:T(8,128)S(1)}, s32[256,256]{1,0:T(8,128)}, u32[]{:S(2)}) copy-start(s32[256,256]{1,0:T(8,128)} %param.7) | copy-start | bytes 786436
  50.2 52.6 %all-to-all-start = ((bf16[16,256,256]{2,1,0:T(8,128)(2,1)}), bf16[16,256,256]{2,1,0:T(8,128)(2,1)S(1)}, u32[]{:S(2)}, u32[]{:S(2)}) async-start(bf16[16,256,256]{2,1,0:T(8,128)(2,1)} %copy-done.1), calls=%async_computation | async-start | bytes 4194304 | tf_op jit(solution)/shard_map/all_to_all | solution.py:334
  56.9 45.8 %copy-start.4 = (f32[2,128,256]{2,1,0:T(8,128)S(1)}, f32[2,128,256]{2,1,0:T(8,128)}, u32[]{:S(2)}) copy-start(f32[2,128,256]{2,1,0:T(8,128)} %gain_ref.1) | copy-start | bytes 786436

commit v2 on v1

--- a/solution.py
+++ b/solution.py
@@ -19,6 +19,10 @@
 PAIRS = RAD // 2
 ROWS = NFFT // PAIRS
 CHAN_BLOCK = 8
+SLOTS = 3
+AHEAD = 4
+SHARES = (3, 1)
+COPIES = 2
 ROT = 16
 MIB = 1 << 20
 
@@ -93,20 +97,23 @@
     return out
 
 
-def spectra_kernel(spec, rows_in, steps_in, pairs, x_ref, halo_ref, win_ref, high_ref, low_ref, out_ref, wide, mid):
+def spectra_kernel(half, blocks, rows_in, steps_in, pairs, x_ref, *refs):
+    halo_refs, (win_ref, high_ref, low_ref) = refs[: half + 1], refs[half + 1 : half + 4]
+    out_refs, (wide, mid) = refs[-2 - len(SHARES) : -2], refs[-2:]
     step = pl.program_id(0)
 
     @pl.when(step < steps_in)
     def _():
-        own = spec * NFFT
-        wide[:, :own] = x_ref[...].astype(jnp.float32)
-        wide[:, own:] = halo_ref[...].astype(jnp.float32)
+        at = 0
+        for ref in (x_ref, *halo_refs):
+            wide[:, at : at + ref.shape[1]] = ref[...].astype(jnp.float32)
+            at += ref.shape[1]
         inputs = rows_in * steps_in
 
         @pl.loop(0, rows_in // 8)
         def _(sub):
             rows = pl.ds(pl.multiple_of(sub * 8, 8), 8)
-            for s in range(spec):
+            for s in range(blocks):
                 vals = []
                 for col in range(RAD):
                     total = None
@@ -126,8 +133,9 @@
     @pl.when(step >= steps_in)
     def _():
         first = (step - steps_in) * pairs
-        owners, _, lanes = out_ref.shape
-        per = ROWS // owners
+        owners, _, lanes = out_refs[0].shape
+        unit = ROWS // owners // sum(SHARES)
+        totals = []
         for p in range(pairs):
             both = mid[first + p]
             high = both.astype(jnp.bfloat16)
@@ -135,39 +143,49 @@
             left = jnp.concatenate([high_ref[p], high_ref[p], low_ref[p]], axis=1)
             right = jnp.concatenate([high, low, high], axis=1)
             total = lax.dot_general(left, right, (((1,), (1,)), ((), ())), preferred_element_type=jnp.float32)
-            out_ref[:, p * per : (p + 1) * per, :] = total.reshape(owners, per, lanes).astype(jnp.bfloat16)
-
-
-def spectra(voltages, halo, owners):
+            totals.append(total.reshape(owners, ROWS // owners, lanes))
+        start = 0
+        for groups, out_ref in zip(SHARES, out_refs):
+            stop = start + groups * unit
+            tile = jnp.concatenate([one[:, start:stop] for one in totals], axis=1)
+            out_ref[...] = tile.astype(jnp.bfloat16)
+            start = stop
+
+
+def spectra(half, voltages, halos, tables, owners, results):
     inputs = voltages.shape[0]
     spec = voltages.shape[1] // NFFT
-    lanes = inputs * spec
+    blocks = spec // 2
+    lanes = inputs * blocks
+    own = spec - half * blocks
+    wanted = (blocks + TAPS - 1) * NFFT - own * NFFT
     rows_in, pairs = 16, 4
     steps_in, steps_out = inputs // rows_in, PAIRS // pairs
-    per = ROWS // owners
-    high, low = second_tables()
+    unit = ROWS // owners // sum(SHARES)
     before = lambda g: jnp.minimum(g, steps_in - 1)
     after = lambda g: jnp.maximum(g - steps_in, 0)
     return pl.pallas_call(
-        functools.partial(spectra_kernel, spec, rows_in, steps_in, pairs),
+        functools.partial(spectra_kernel, half, blocks, rows_in, steps_in, pairs),
         grid=(steps_in + steps_out,),
-        in_specs=[
-            pl.BlockSpec((rows_in, spec * NFFT), lambda g: (before(g), 0)),
-            pl.BlockSpec((rows_in, (TAPS - 1) * NFFT), lambda g: (before(g), 0)),
+        in_specs=[pl.BlockSpec((rows_in, own * NFFT), lambda g: (before(g), half))]
+        + [pl.BlockSpec((rows_in, min(wanted, halo.shape[1])), lambda g: (before(g), 0)) for halo in halos]
+        + [
             pl.BlockSpec((TAPS, NFFT), lambda g: (0, 0)),
             pl.BlockSpec((pairs, ROWS, 2 * LANES), lambda g: (after(g), 0, 0)),
             pl.BlockSpec((pairs, ROWS, 2 * LANES), lambda g: (after(g), 0, 0)),
-        ],
-        out_specs=pl.BlockSpec((owners, pairs * per, lanes), lambda g: (0, after(g), 0)),
-        out_shape=jax.ShapeDtypeStruct((owners, PAIRS * per, lanes), jnp.bfloat16),
+        ]
+        + [pl.BlockSpec(memory_space=pl.ANY)] * len(results),
+        out_specs=[pl.BlockSpec((owners, pairs * unit * n, lanes), lambda g: (0, after(g), half)) for n in SHARES],
+        out_shape=[jax.ShapeDtypeStruct((owners, PAIRS * unit * n, inputs * spec), jnp.bfloat16) for n in SHARES],
+        input_output_aliases={len(halos) + 4 + i: i for i in range(len(results))},
         scratch_shapes=[
-            pltpu.VMEM((rows_in, (spec + TAPS - 1) * NFFT), jnp.float32),
+            pltpu.VMEM((rows_in, (blocks + TAPS - 1) * NFFT), jnp.float32),
             pltpu.VMEM((PAIRS, lanes, 2 * LANES), jnp.float32),
         ],
-        compiler_params=pltpu.CompilerParams(vmem_limit_bytes=40 * MIB),
-        cost_estimate=pl.CostEstimate(flops=6 * PAIRS * ROWS * 256 * lanes, bytes_accessed=12 * MIB, transcendentals=0),
+        compiler_params=pltpu.CompilerParams(vmem_limit_bytes=20 * MIB),
+        cost_estimate=pl.CostEstimate(flops=6 * PAIRS * ROWS * 256 * lanes, bytes_accessed=8 * MIB, transcendentals=0),
         name="spectra",
-    )(voltages, halo, jnp.asarray(window_table()), jnp.asarray(high), jnp.asarray(low))
+    )(voltages, *halos, *tables, *results)
 
 
 def unit_circle(phase):
@@ -220,20 +238,55 @@
     )(chan_first.reshape(1), beam_delays.T)
 
 
-def combine_kernel(tm_count, spec, inputs, g_ref, gain_ref, w_ref, vis_ref, power_ref, rows_ref):
+def combine_kernel(tm_count, spec, inputs, share, out_steps, g_ref, gain_ref, w_ref, *refs):
+    (vis_ref, power_ref, rows_ref, held, sems, ahead, w_sems) = refs[-7:]
     step = pl.program_id(0)
+    steps = pl.num_programs(0)
+    before = sum(SHARES[:share]) * (RAD // CHAN_BLOCK)
+    slot = step % SLOTS
+
+    def vis_copies(at_step):
+        at = at_step % SLOTS
+        wide = CHAN_BLOCK // COPIES
+        for part in range(2):
+            for c in range(COPIES):
+                yield pltpu.make_async_copy(
+                    held.at[at, part, pl.ds(c * wide, wide)],
+                    vis_ref.at[part, pl.ds((before + at_step) * CHAN_BLOCK + c * wide, wide)],
+                    sems.at[at, part, c],
+                )
+
+    def weight_copy(at_step):
+        at = at_step % AHEAD
+        return pltpu.make_async_copy(w_ref.at[pl.ds((before + at_step) * CHAN_BLOCK, CHAN_BLOCK)], ahead.at[at], w_sems.at[at])
+
+    @pl.when(step == 0)
+    def _():
+        for first in range(min(AHEAD - 1, out_steps)):
+            weight_copy(first).start()
+
+    @pl.when(step + AHEAD - 1 < out_steps)
+    def _():
+        weight_copy(step + AHEAD - 1).start()
+
+    @pl.when(step >= SLOTS)
+    def _():
+        for copy in vis_copies(step - SLOTS):
+            copy.wait()
+
     rows = g_ref.shape[1]
     per = rows // PAIRS
+    tile = 16
     times = tm_count * spec
     half = LANES // 2
 
     @pl.when(step == 0)
     def _():
-        low_half = lax.broadcasted_iota(jnp.int32, (per, LANES), 1) < half
-
-        @pl.loop(0, PAIRS)
+        low_half = lax.broadcasted_iota(jnp.int32, (tile, LANES), 1) < half
+
+        @pl.loop(0, rows // tile)
         def _(m):
-            at = pl.ds(pl.multiple_of(m * per, per), per)
+            at = pl.ds(pl.multiple_of(m * tile, tile), tile)
             for t in range(tm_count):
                 for pair in range(2):
                     for two in range(2):
@@ -243,13 +296,13 @@
                         even = jnp.where(low_half, a, pltpu.roll(b, half, 1))
                         odd = jnp.where(low_half, pltpu.roll(a, half, 1), b)
                         s = t * spec + 2 * two
-                        rows_ref[pair, pl.ds(pl.multiple_of(s * rows + m * per, per), per), :] = even
-                        rows_ref[pair, pl.ds(pl.multiple_of((s + 1) * rows + m * per, per), per), :] = odd
-
+                        rows_ref[pair, pl.ds(pl.multiple_of(s * rows + m * tile, tile), tile), :] = even
+                        rows_ref[pair, pl.ds(pl.multiple_of((s + 1) * rows + m * tile, tile), tile), :] = odd
+
+    weight_copy(step).wait()
     scale = 1.0 / times
     blocks = RAD // CHAN_BLOCK
     for u in range(CHAN_BLOCK):
-        k = step * CHAN_BLOCK + u
         k2 = (step % blocks) * CHAN_BLOCK + u
         upper = k2 // PAIRS
         m = jnp.where(k2 == PAIRS, 0, jnp.where(upper == 1, RAD - k2, k2))
@@ -265,44 +318,62 @@
         both = jnp.concatenate([stacked, turned], axis=1)
         vis = lax.dot_general(stacked, both, (((0,), (0,)), ((), ())), preferred_element_type=jnp.float32)
         vis = (vis * scale).astype(jnp.bfloat16)
-        vis_ref[0, u] = vis[:, :inputs]
-        vis_ref[1, u] = vis[:, inputs:]
+        held[slot, 0, u] = vis[:, :inputs]
+        held[slot, 1, u] = vis[:, inputs:]
         left = jnp.concatenate([stacked, turned], axis=1)
-        w = w_ref[u].reshape(2 * inputs, w_ref.shape[3])
+        w = ahead[step % AHEAD, u].reshape(2 * inputs, w_ref.shape[3])
         formed = lax.dot_general(left, w, (((1,), (0,)), ((), ())), preferred_element_type=jnp.float32)
         formed = formed * formed
         power_ref[u] = (formed[:times] + formed[times:]).astype(jnp.bfloat16)
 
-
-def combine(gathered, cal_gains, weights, tm_count, spec):
+    for copy in vis_copies(step):
+        copy.start()
+
+    @pl.when(step == steps - 1)
+    def _():
+        for back in range(min(SLOTS, out_steps) - 1, -1, -1):
+            for copy in vis_copies(step - back):
+                copy.wait()
+
+
+def combine(gathered, cal_gains, weights, tm_count, spec, share, results):
     sources, rows, lanes = gathered.shape
     chan_local, _, inputs, beams = weights.shape
     times = tm_count * spec
+    steps = SHARES[share] * (RAD // CHAN_BLOCK)
+    first = sum(SHARES[:share]) * (RAD // CHAN_BLOCK)
     return pl.pallas_call(
-        functools.partial(combine_kernel, tm_count, spec, inputs),
-        grid=(chan_local // CHAN_BLOCK,),
+        functools.partial(combine_kernel, tm_count, spec, inputs, share, steps),
+        grid=(steps,),
         in_specs=[
             pl.BlockSpec((sources, rows, lanes), lambda g: (0, 0, 0)),
-            pl.BlockSpec((2, CHAN_BLOCK, inputs), lambda g: (0, g, 0)),
-            pl.BlockSpec((CHAN_BLOCK, 2, inputs, beams), lambda g: (g, 0, 0, 0)),
-        ],
+            pl.BlockSpec((2, CHAN_BLOCK, inputs), lambda g: (0, first + g, 0)),
+        ]
+        + [pl.BlockSpec(memory_space=pl.ANY)] * (1 + len(results)),
+        input_output_aliases={3 + i: i for i in range(len(results))},
         out_specs=[
-            pl.BlockSpec((2, CHAN_BLOCK, inputs, inputs), lambda g: (0, g, 0, 0)),
-            pl.BlockSpec((CHAN_BLOCK, times, beams), lambda g: (g, 0, 0)),
+            pl.BlockSpec(memory_space=pl.ANY),
+            pl.BlockSpec((CHAN_BLOCK, times, beams), lambda g: (first + g, 0, 0)),
         ],
         out_shape=[
             jax.ShapeDtypeStruct((2, chan_local, inputs, inputs), jnp.bfloat16),
             jax.ShapeDtypeStruct((chan_local, times, beams), jnp.bfloat16),
         ],
-        scratch_shapes=[pltpu.VMEM((2, times * rows, LANES), jnp.float32)],
-        compiler_params=pltpu.CompilerParams(vmem_limit_bytes=40 * MIB),
+        scratch_shapes=[
+            pltpu.VMEM((2, times * rows, LANES), jnp.float32),
+            pltpu.VMEM((SLOTS, 2, CHAN_BLOCK, inputs, inputs), jnp.bfloat16),
+            pltpu.SemaphoreType.DMA((SLOTS, 2, COPIES)),
+            pltpu.VMEM((AHEAD, CHAN_BLOCK, 2, inputs, beams), jnp.bfloat16),
+            pltpu.SemaphoreType.DMA((AHEAD,)),
+        ],
+        compiler_params=pltpu.CompilerParams(vmem_limit_bytes=28 * MIB),
         cost_estimate=pl.CostEstimate(
-            flops=chan_local * (4 * 2 * times * inputs * inputs + 8 * times * inputs * beams),
-            bytes_accessed=chan_local * (4 * inputs * inputs + 4 * inputs * beams),
+            flops=steps * CHAN_BLOCK * (4 * 2 * times * inputs * inputs + 8 * times * inputs * beams),
+            bytes_accessed=steps * CHAN_BLOCK * (4 * inputs * inputs + 4 * inputs * beams),
             transcendentals=0,
         ),
         name="combine",
-    )(gathered, cal_gains, weights)
+    )(gathered, cal_gains, weights, *results)
 
 
 def fits(voltages, beam_delays, tm_count, chan_count):
@@ -312,6 +383,7 @@
     return (
         ROWS % owners == 0
         and ROWS // owners == 16
+        and CH // owners == sum(SHARES) * RAD
         and spec == 4
         and chan_count == 4
         and inp_dev * 2 == LANES
@@ -327,12 +399,22 @@
     owners = tm_count * chan_count
     chan_local = CH // owners
     spec_dev = voltages.shape[1] // NFFT
-    halo = shifted(voltages[:, : (TAPS - 1) * NFFT].astype(jnp.bfloat16), "tm", -1)
+    early = shifted(voltages[:, : 2 * NFFT].astype(jnp.bfloat16), "tm", -1)
+    late = shifted(voltages[:, 2 * NFFT : (TAPS - 1) * NFFT].astype(jnp.bfloat16), "tm", -1)
     chan_first = (lax.axis_index("tm") * chan_count + lax.axis_index("chan")) * chan_local
     weights = beam_weights(beam_delays, chan_first, chan_local)
-    sent = spectra(voltages, halo, owners)
-    gathered = lax.all_to_all(sent, ("tm", "chan"), split_axis=0, concat_axis=0, tiled=True)
-    visibilities, beam_power = combine(gathered, cal_gains, weights, tm_count, spec_dev)
+    tables = [jnp.asarray(table) for table in (window_table(), *second_tables())]
+    sent = spectra(0, voltages, [early], tables, owners, ())
+    sent = spectra(1, voltages, [early, late], tables, owners, sent)
+    results = ()
+    for share in range(len(SHARES)):
+        if share:
+            block, gathered, weights = lax.optimization_barrier((sent[share], gathered, weights))
+            results = combine(gathered, cal_gains, weights, tm_count, spec_dev, share - 1, results)
+        else:
+            block = sent[share]
+        gathered = lax.all_to_all(block, ("tm", "chan"), split_axis=0, concat_axis=0, tiled=True)
+    visibilities, beam_power = combine(gathered, cal_gains, weights, tm_count, spec_dev, len(SHARES) - 1, results)
     return (visibilities, beam_power)
 
 

time: 140 us -> 122 us (0.87)
  waiting for transfers between devices: 62.3 us -> 44.8 us
  starting transfers between devices: 8.62 us -> 16.3 us
  local copies, waits for them, and re-layouts: 4.65 us -> 0.27 us
  Pallas kernels: 59.7 us -> 55.9 us
    all_to_all x1 -> x2, waiting for transfers between devices: 27.1 us -> 16.6 us  [shards(): lax.all_to_all(block, ('tm', 'chan'), split_axis=0, concat_axis=0, tiled=...]
    ppermute x1 -> x2, waiting for transfers between devices: 35.2 us -> 28.2 us  [shifted(): return lax.ppermute(block, axis, route)]
    all_to_all x1 -> x2, starting transfers between devices: 6.57 us -> 12.2 us  [shards(): lax.all_to_all(block, ('tm', 'chan'), split_axis=0, concat_axis=0, tiled=...]
    unnamed x15 -> x13, local copies, waits for them, and re-layouts: 4.65 us -> 0.16 us
    pallas_call x2 -> x4, Pallas kernels: 40.9 us -> 37.1 us  [the longest x2 27 us: combine(): pl.pallas_call(functools.partial(combine_kernel, tm_count, spec, inputs,...]
    ppermute x1 -> x2, starting transfers between devices: 2.05 us -> 4.1 us  [shifted(): return lax.ppermute(block, axis, route)]
  transfers between devices with their start and end apart: 2 -> 4, of which waited for: 2 -> 3; matrix products, arithmetic and copies ran while one was open for 0% -> 0% of each run, Pallas kernels for 14% -> 35%
where the time goes in v2:
time: 122 us; the launch traced here: 121 us
  Pallas kernels  55.9 us (46%)
  waiting for transfers between devices  44.8 us (37%)
  starting transfers between devices  16.3 us (13%)
  other arithmetic  2.54 us (2%)
    ppermute x2, waiting for transfers between devices, shifted(): return lax.ppermute(block, axis, route)  28.2 us
    pallas_call x2, Pallas kernels, combine(): pl.pallas_call(functools.partial(combine_kernel, tm_count, spec, inputs,...  27 us
    pallas_call x1, Pallas kernels, beam_weights(): pl.pallas_call(functools.partial(weights_kernel, 1.0 / math.sqrt(inputs))...  18.7 us
    all_to_all x2, waiting for transfers between devices, shards(): lax.all_to_all(block, ('tm', 'chan'), split_axis=0, concat_axis=0, tiled=...  16.6 us
    all_to_all x2, starting transfers between devices, shards(): lax.all_to_all(block, ('tm', 'chan'), split_axis=0, concat_axis=0, tiled=...  12.2 us
    pallas_call x2, Pallas kernels, spectra(): pl.pallas_call(functools.partial(spectra_kernel, half, blocks, rows_in, s...  10.2 us
    ppermute x2, starting transfers between devices, shifted(): return lax.ppermute(block, axis, route)  4.1 us
    another operation x1, other arithmetic  2.54 us
  transfers between devices with their start and end apart: 4, of which 3 were waited for; matrix products, arithmetic and copies ran while one was open for 0% of the time, Pallas kernels for 35%

profile of v2, /device:TPU:9, one launch (start us, length us, event | category | flops | bytes accessed | tf_op | source)
XLA Modules:
  0.0 120.5 jit_solution(16605818352050089304)
XLA Ops:
  0.6 0.0 copy-start
  0.6 0.0 copy-start.2
  0.7 2.5 %convert.4 = bf16[64,16384]{1,0:T(8,128)(2,1)S(1)} convert(s32[64,16384]{1,0:T(8,128)} %x_ref.3) | non-fusion elementwise | flops 1048576 | bytes 6291456 | tf_op jit(solution)/shard_map/convert.1
  3.2 0.0 copy-start.1
  3.2 0.0 copy-start.4
  3.2 0.1 slice.10
  3.3 2.2 %collective-permute-start = (bf16[64,8192]{1,0:T(8,128)(2,1)S(1)}, bf16[64,8192]{1,0:T(8,128)(2,1)S(1)}, u32[]{:S(2)}, u32[]{:S(2)}) collective-permute-start(bf16[64,8192]{1,0:T(8,128)(2,1)S(1)} %slice.10), channel_id=1, source_target_pairs={{4,0},{8,4},{12,8},{5,1},{9,5},{13,9},{6,2},{10,6},{14,10},{7,3},{... | collective-permute-start | bytes 3145736 | tf_op jit(solution)/shard_map/ppermute | solution.py:33
  5.5 1.9 %collective-permute-start.1 = (bf16[64,4096]{1,0:T(8,128)(2,1)S(1)}, bf16[64,4096]{1,0:T(8,128)(2,1)S(1)}, u32[]{:S(2)}, u32[]{:S(2)}) collective-permute-start(bf16[64,4096]{1,0:T(8,128)(2,1)S(1)} %slice.11), channel_id=1, source_target_pairs={{4,0},{8,4},{12,8},{5,1},{9,5},{13,9},{6,2},{10,6},{14,10},{7,3},{... | collective-permute-start | bytes 1572872 | tf_op jit(solution)/shard_map/ppermute | solution.py:33
  7.5 22.0 %collective-permute-done.refs_0_ = bf16[64,8192]{1,0:T(8,128)(2,1)S(1)} collective-permute-done((bf16[64,8192]{1,0:T(8,128)(2,1)S(1)}, bf16[64,8192]{1,0:T(8,128)(2,1)S(1)}, u32[]{:S(2)}, u32[]{:S(2)}) %collective-permute-start) | collective-permute-done | bytes 1048608 | tf_op jit(solution)/shard_map/ppermute | solution.py:33
  29.5 0.0 copy-done
  29.5 0.0 copy-done.2
  29.5 0.0 copy-done.1
  29.5 0.0 copy-done.4
  29.5 5.0 %spectra.2 = (bf16[16,192,256]{2,1,0:T(8,128)(2,1)}, bf16[16,64,256]{2,1,0:T(8,128)(2,1)}) custom-call(s32[64,16384]{1,0:T(8,128)S(1)} %copy-done, bf16[64,8192]{1,0:T(8,128)(2,1)S(1)} %collective-permute-done.refs_0_, f32[4,4096]{1,0:T(4,128)S(1)} %copy-done.4, bf16[16,256,256]{2,1,0:T(8,128)(2,1)S(1)} %copy-done.2, bf16[16,256,256]{2,1,0:T(8,128)(2,1)S(1)} %copy-done.1), custom_call_target="tpu_custom_call" | custom-call | flops 805306368 | bytes 8388608 | tf_op jit(solution)/shard_map/spectra/pallas_call | solution.py:167
  34.5 6.2 %collective-permute-done.1.refs_1_ = bf16[64,4096]{1,0:T(8,128)(2,1)S(1)} collective-permute-done((bf16[64,4096]{1,0:T(8,128)(2,1)S(1)}, bf16[64,4096]{1,0:T(8,128)(2,1)S(1)}, u32[]{:S(2)}, u32[]{:S(2)}) %collective-permute-start.1) | collective-permute-done | bytes 524320 | tf_op jit(solution)/shard_map/ppermute | solution.py:33
  40.7 5.2 %spectra.3 = (bf16[16,192,256]{2,1,0:T(8,128)(2,1)}, bf16[16,64,256]{2,1,0:T(8,128)(2,1)}) custom-call(s32[64,16384]{1,0:T(8,128)S(1)} %copy-done, bf16[64,8192]{1,0:T(8,128)(2,1)S(1)} %collective-permute-done.refs_0_, bf16[64,4096]{1,0:T(8,128)(2,1)S(1)} %collective-permute-done.1.refs_1_, ...), custom_call_target="tpu_custom_call", output_to_operand_aliasing={{0}: (6, {}), {1}: (7, {})} | custom-call | flops 805306368 | bytes 8388608 | tf_op jit(solution)/shard_map/spectra/pallas_call | solution.py:167
  45.9 0.0 copy-start.5
  45.9 6.6 %all-to-all-start = ((bf16[16,192,256]{2,1,0:T(8,128)(2,1)}), bf16[16,192,256]{2,1,0:T(8,128)(2,1)S(1)}, u32[]{:S(2)}, u32[]{:S(2)}) async-start(bf16[16,192,256]{2,1,0:T(8,128)(2,1)} %get-tuple-element.14), calls=%async_computation | async-start | bytes 3145728 | tf_op jit(solution)/shard_map/all_to_all | solution.py:416
  52.5 0.0 copy-done.5
  52.5 0.1 copy.12
  52.6 0.0 copy-start.3
  52.6 18.7 %weights.1.w_ref = bf16[128,2,256,256]{3,2,1,0:T(8,128)(2,1)} custom-call(s32[1]{0:T(128)} %bitcast.first_ref, s32[256,256]{1,0:T(8,128)S(1)} %bitcast.2), custom_call_target="tpu_custom_call" | custom-call | flops 503316480 | bytes 33554432 | tf_op jit(solution)/shard_map/weights/pallas_call | solution.py:224
  71.3 16.6 %all-to-all-done.g_ref = bf16[16,192,256]{2,1,0:T(8,128)(2,1)S(1)} async-done(((bf16[16,192,256]{2,1,0:T(8,128)(2,1)}), bf16[16,192,256]{2,1,0:T(8,128)(2,1)S(1)}, u32[]{:S(2)}, u32[]{:S(2)}) %all-to-all-start) | async-done | bytes 1572896 | tf_op jit(solution)/shard_map/all_to_all | solution.py:416
  87.9 5.6 %all-to-all-start.1 = ((bf16[16,64,256]{2,1,0:T(8,128)(2,1)}), bf16[16,64,256]{2,1,0:T(8,128)(2,1)S(1)}, u32[]{:S(2)}, u32[]{:S(2)}) async-start(bf16[16,64,256]{2,1,0:T(8,128)(2,1)} %get-tuple-element.15), calls=%async_computation.1 | async-start | bytes 1048576 | tf_op jit(solution)/shard_map/all_to_all | solution.py:416
  93.5 0.0 copy-done.3
  93.6 19.0 %combine.2 = (bf16[2,128,256,256]{3,2,1,0:T(8,128)(2,1)}, bf16[128,16,256]{2,1,0:T(8,128)(2,1)}) custom-call(bf16[16,192,256]{2,1,0:T(8,128)(2,1)S(1)} %all-to-all-done.g_ref, f32[2,128,256]{2,1,0:T(8,128)S(1)} %copy-done.3, bf16[128,2,256,256]{3,2,1,0:T(8,128)(2,1)} %weights.1.w_ref), custom_call_target="tpu_custom_call" | custom-call | flops 1610612736 | bytes 50331648 | tf_op jit(solution)/shard_map/combine/pallas_call | solution.py:345
  112.6 0.0 all-to-all-done.1.g_ref
  112.6 7.9 %combine.3 = (bf16[2,128,256,256]{3,2,1,0:T(8,128)(2,1)}, bf16[128,16,256]{2,1,0:T(8,128)(2,1)}) custom-call(bf16[16,64,256]{2,1,0:T(8,128)(2,1)S(1)} %all-to-all-done.1.g_ref, f32[2,128,256]{2,1,0:T(8,128)S(1)} %copy-done.3, bf16[128,2,256,256]{3,2,1,0:T(8,128)(2,1)} %weights.1.w_ref, ...), custom_call_target="tpu_custom_call", output_to_operand_aliasing={{0}: (3, {}), {1}: (4, {})} | custom-call | flops 536870912 | bytes 16777216 | tf_op jit(solution)/shard_map/combine/pallas_call | solution.py:345
  (1 shorter events, 0.0 us)
Async XLA Ops:
  0.6 28.9 %copy-start = (s32[64,16384]{1,0:T(8,128)S(1)}, s32[64,16384]{1,0:T(8,128)}, u32[]{:S(2)}) copy-start(s32[64,16384]{1,0:T(8,128)} %x_ref.3) | copy-start | bytes 12582916
  0.6 28.9 %copy-start.2 = (bf16[16,256,256]{2,1,0:T(8,128)(2,1)S(1)}, bf16[16,256,256]{2,1,0:T(8,128)(2,1)}, u32[]{:S(2)}) copy-start(bf16[16,256,256]{2,1,0:T(8,128)(2,1)} %constant.18.clone.refs_2_.refs_3_) | copy-start | bytes 6291460
  3.2 26.3 %copy-start.1 = (bf16[16,256,256]{2,1,0:T(8,128)(2,1)S(1)}, bf16[16,256,256]{2,1,0:T(8,128)(2,1)}, u32[]{:S(2)}) copy-start(bf16[16,256,256]{2,1,0:T(8,128)(2,1)} %constant.19.clone.refs_3_.refs_4_) | copy-start | bytes 6291460
  3.2 26.3 %copy-start.4 = (f32[4,4096]{1,0:T(4,128)S(1)}, f32[4,4096]{1,0:T(4,128)}, u32[]{:S(2)}) copy-start(f32[4,4096]{1,0:T(4,128)} %constant.17.clone.refs_1_.refs_2_) | copy-start | bytes 196612
  3.3 26.2 %collective-permute-start = (bf16[64,8192]{1,0:T(8,128)(2,1)S(1)}, bf16[64,8192]{1,0:T(8,128)(2,1)S(1)}, u32[]{:S(2)}, u32[]{:S(2)}) collective-permute-start(bf16[64,8192]{1,0:T(8,128)(2,1)S(1)} %slice.10), channel_id=1, source_target_pairs={{4,0},{8,4},{12,8},{5,1},{9,5},{13,9},{6,2},{10,6},{14,10},{7,3},{... | collective-permute-start | bytes 3145736 | tf_op jit(solution)/shard_map/ppermute | solution.py:33
  5.5 35.2 %collective-permute-start.1 = (bf16[64,4096]{1,0:T(8,128)(2,1)S(1)}, bf16[64,4096]{1,0:T(8,128)(2,1)S(1)}, u32[]{:S(2)}, u32[]{:S(2)}) collective-permute-start(bf16[64,4096]{1,0:T(8,128)(2,1)S(1)} %slice.11), channel_id=1, source_target_pairs={{4,0},{8,4},{12,8},{5,1},{9,5},{13,9},{6,2},{10,6},{14,10},{7,3},{... | collective-permute-start | bytes 1572872 | tf_op jit(solution)/shard_map/ppermute | solution.py:33
  45.9 6.6 %copy-start.5 = (s32[256,256]{1,0:T(8,128)S(1)}, s32[256,256]{1,0:T(8,128)}, u32[]{:S(2)}) copy-start(s32[256,256]{1,0:T(8,128)} %param.7) | copy-start | bytes 786436
  45.9 42.0 %all-to-all-start = ((bf16[16,192,256]{2,1,0:T(8,128)(2,1)}), bf16[16,192,256]{2,1,0:T(8,128)(2,1)S(1)}, u32[]{:S(2)}, u32[]{:S(2)}) async-start(bf16[16,192,256]{2,1,0:T(8,128)(2,1)} %get-tuple-element.14), calls=%async_computation | async-start | bytes 3145728 | tf_op jit(solution)/shard_map/all_to_all | solution.py:416
  52.6 40.9 %copy-start.3 = (f32[2,128,256]{2,1,0:T(8,128)S(1)}, f32[2,128,256]{2,1,0:T(8,128)}, u32[]{:S(2)}) copy-start(f32[2,128,256]{2,1,0:T(8,128)} %gain_ref.3) | copy-start | bytes 786436
  87.9 24.7 %all-to-all-start.1 = ((bf16[16,64,256]{2,1,0:T(8,128)(2,1)}), bf16[16,64,256]{2,1,0:T(8,128)(2,1)S(1)}, u32[]{:S(2)}, u32[]{:S(2)}) async-start(bf16[16,64,256]{2,1,0:T(8,128)(2,1)} %get-tuple-element.15), calls=%async_computation.1 | async-start | bytes 1048576 | tf_op jit(solution)/shard_map/all_to_all | solution.py:416

commit v3 on v2

--- a/solution.py
+++ b/solution.py
@@ -21,7 +21,8 @@
 CHAN_BLOCK = 8
 SLOTS = 3
 AHEAD = 4
-SHARES = (3, 1)
+SHARES = (5, 3)
+GROUP = RAD // 2
 COPIES = 2
 ROT = 16
 MIB = 1 << 20
@@ -242,7 +243,7 @@
     (vis_ref, power_ref, rows_ref, held, sems, ahead, w_sems) = refs[-7:]
     step = pl.program_id(0)
     steps = pl.num_programs(0)
-    before = sum(SHARES[:share]) * (RAD // CHAN_BLOCK)
+    before = sum(SHARES[:share]) * (GROUP // CHAN_BLOCK)
     slot = step % SLOTS
 
     def vis_copies(at_step):
@@ -303,10 +304,10 @@
     scale = 1.0 / times
     blocks = RAD // CHAN_BLOCK
     for u in range(CHAN_BLOCK):
-        k2 = (step % blocks) * CHAN_BLOCK + u
+        k2 = ((before + step) % blocks) * CHAN_BLOCK + u
         upper = k2 // PAIRS
         m = jnp.where(k2 == PAIRS, 0, jnp.where(upper == 1, RAD - k2, k2))
-        row = m * per + (step // blocks) * 4 + upper * 2
+        row = m * per + ((before + step) // blocks) * 4 + upper * 2 - 2 * sum(SHARES[:share])
         z_re = jnp.concatenate([rows_ref[p, pl.ds(row, times, stride=rows), :] for p in range(2)], axis=1)
         z_im = jnp.concatenate([rows_ref[p, pl.ds(row + 1, times, stride=rows), :] for p in range(2)], axis=1)
         g_re = gain_ref[0, u : u + 1, :]
@@ -340,8 +341,8 @@
     sources, rows, lanes = gathered.shape
     chan_local, _, inputs, beams = weights.shape
     times = tm_count * spec
-    steps = SHARES[share] * (RAD // CHAN_BLOCK)
-    first = sum(SHARES[:share]) * (RAD // CHAN_BLOCK)
+    steps = SHARES[share] * (GROUP // CHAN_BLOCK)
+    first = sum(SHARES[:share]) * (GROUP // CHAN_BLOCK)
     return pl.pallas_call(
         functools.partial(combine_kernel, tm_count, spec, inputs, share, steps),
         grid=(steps,),
@@ -383,7 +384,7 @@
     return (
         ROWS % owners == 0
         and ROWS // owners == 16
-        and CH // owners == sum(SHARES) * RAD
+        and CH // owners == sum(SHARES) * GROUP
         and spec == 4
         and chan_count == 4
         and inp_dev * 2 == LANES

time: 122 us -> 118 us (0.967); the launches traced: 121 us -> 118 us
  waiting for transfers between devices: 44.8 us -> 43 us
    all_to_all x2, waiting for transfers between devices: 16.6 us -> 14.9 us  [shards(): lax.all_to_all(block, ('tm', 'chan'), split_axis=0, concat_axis=0, tiled=...]
  transfers between devices with their start and end apart: 4 -> 4, of which waited for: 3 -> 4; matrix products, arithmetic and copies ran while one was open for 0% -> 0% of each run, Pallas kernels for 35% -> 34%
where the time goes in v3:
time: 118 us
  Pallas kernels  55.4 us (47%)
  waiting for transfers between devices  43 us (36%)
  starting transfers between devices  15.9 us (13%)
  other arithmetic  2.54 us (2%)
    ppermute x2, waiting for transfers between devices, shifted(): return lax.ppermute(block, axis, route)  28.2 us
    pallas_call x2, Pallas kernels, combine(): pl.pallas_call(functools.partial(combine_kernel, tm_count, spec, inputs,...  26.5 us
    pallas_call x1, Pallas kernels, beam_weights(): pl.pallas_call(functools.partial(weights_kernel, 1.0 / math.sqrt(inputs))...  18.7 us
    all_to_all x2, waiting for transfers between devices, shards(): lax.all_to_all(block, ('tm', 'chan'), split_axis=0, concat_axis=0, tiled=...  14.9 us
    all_to_all x2, starting transfers between devices, shards(): lax.all_to_all(block, ('tm', 'chan'), split_axis=0, concat_axis=0, tiled=...  11.8 us
    pallas_call x2, Pallas kernels, spectra(): pl.pallas_call(functools.partial(spectra_kernel, half, blocks, rows_in, s...  10.2 us
    ppermute x2, starting transfers between devices, shifted(): return lax.ppermute(block, axis, route)  4.1 us
    another operation x1, other arithmetic  2.54 us
  transfers between devices with their start and end apart: 4, of which 4 were waited for; matrix products, arithmetic and copies ran while one was open for 0% of the time, Pallas kernels for 34%

profile of v3, /device:TPU:9, one launch (start us, length us, event | category | flops | bytes accessed | tf_op | source)
XLA Modules:
  0.0 117.9 jit_solution(3452113509270655515)
XLA Ops:
  0.6 0.0 copy-start
  0.6 0.0 copy-start.2
  0.7 2.5 %convert.4 = bf16[64,16384]{1,0:T(8,128)(2,1)S(1)} convert(s32[64,16384]{1,0:T(8,128)} %x_ref.3) | non-fusion elementwise | flops 1048576 | bytes 6291456 | tf_op jit(solution)/shard_map/convert.1
  3.2 0.0 copy-start.1
  3.2 0.0 copy-start.4
  3.2 0.1 slice.10
  3.3 2.2 %collective-permute-start = (bf16[64,8192]{1,0:T(8,128)(2,1)S(1)}, bf16[64,8192]{1,0:T(8,128)(2,1)S(1)}, u32[]{:S(2)}, u32[]{:S(2)}) collective-permute-start(bf16[64,8192]{1,0:T(8,128)(2,1)S(1)} %slice.10), channel_id=1, source_target_pairs={{4,0},{8,4},{12,8},{5,1},{9,5},{13,9},{6,2},{10,6},{14,10},{7,3},{... | collective-permute-start | bytes 3145736 | tf_op jit(solution)/shard_map/ppermute | solution.py:34
  5.5 1.9 %collective-permute-start.1 = (bf16[64,4096]{1,0:T(8,128)(2,1)S(1)}, bf16[64,4096]{1,0:T(8,128)(2,1)S(1)}, u32[]{:S(2)}, u32[]{:S(2)}) collective-permute-start(bf16[64,4096]{1,0:T(8,128)(2,1)S(1)} %slice.11), channel_id=1, source_target_pairs={{4,0},{8,4},{12,8},{5,1},{9,5},{13,9},{6,2},{10,6},{14,10},{7,3},{... | collective-permute-start | bytes 1572872 | tf_op jit(solution)/shard_map/ppermute | solution.py:34
  7.5 22.0 %collective-permute-done.refs_0_ = bf16[64,8192]{1,0:T(8,128)(2,1)S(1)} collective-permute-done((bf16[64,8192]{1,0:T(8,128)(2,1)S(1)}, bf16[64,8192]{1,0:T(8,128)(2,1)S(1)}, u32[]{:S(2)}, u32[]{:S(2)}) %collective-permute-start) | collective-permute-done | bytes 1048608 | tf_op jit(solution)/shard_map/ppermute | solution.py:34
  29.5 0.0 copy-done
  29.5 0.0 copy-done.2
  29.5 0.0 copy-done.1
  29.5 0.0 copy-done.4
  29.5 5.1 %spectra.2 = (bf16[16,160,256]{2,1,0:T(8,128)(2,1)}, bf16[16,96,256]{2,1,0:T(8,128)(2,1)}) custom-call(s32[64,16384]{1,0:T(8,128)S(1)} %copy-done, bf16[64,8192]{1,0:T(8,128)(2,1)S(1)} %collective-permute-done.refs_0_, f32[4,4096]{1,0:T(4,128)S(1)} %copy-done.4, bf16[16,256,256]{2,1,0:T(8,128)(2,1)S(1)} %copy-done.2, bf16[16,256,256]{2,1,0:T(8,128)(2,1)S(1)} %copy-done.1), custom_call_target="tpu_custom_call" | custom-call | flops 805306368 | bytes 8388608 | tf_op jit(solution)/shard_map/spectra/pallas_call | solution.py:168
  34.6 6.2 %collective-permute-done.1.refs_1_ = bf16[64,4096]{1,0:T(8,128)(2,1)S(1)} collective-permute-done((bf16[64,4096]{1,0:T(8,128)(2,1)S(1)}, bf16[64,4096]{1,0:T(8,128)(2,1)S(1)}, u32[]{:S(2)}, u32[]{:S(2)}) %collective-permute-start.1) | collective-permute-done | bytes 524320 | tf_op jit(solution)/shard_map/ppermute | solution.py:34
  40.7 5.1 %spectra.3 = (bf16[16,160,256]{2,1,0:T(8,128)(2,1)}, bf16[16,96,256]{2,1,0:T(8,128)(2,1)}) custom-call(s32[64,16384]{1,0:T(8,128)S(1)} %copy-done, bf16[64,8192]{1,0:T(8,128)(2,1)S(1)} %collective-permute-done.refs_0_, bf16[64,4096]{1,0:T(8,128)(2,1)S(1)} %collective-permute-done.1.refs_1_, ...), custom_call_target="tpu_custom_call", output_to_operand_aliasing={{0}: (6, {}), {1}: (7, {})} | custom-call | flops 805306368 | bytes 8388608 | tf_op jit(solution)/shard_map/spectra/pallas_call | solution.py:168
  45.9 0.0 copy-start.5
  45.9 6.6 %all-to-all-start = ((bf16[16,160,256]{2,1,0:T(8,128)(2,1)}), bf16[16,160,256]{2,1,0:T(8,128)(2,1)S(1)}, u32[]{:S(2)}, u32[]{:S(2)}) async-start(bf16[16,160,256]{2,1,0:T(8,128)(2,1)} %get-tuple-element.14), calls=%async_computation | async-start | bytes 2621440 | tf_op jit(solution)/shard_map/all_to_all | solution.py:417
  52.4 0.0 copy-done.5
  52.5 0.1 copy.12
  52.6 0.0 copy-start.3
  52.6 18.7 %weights.1.w_ref = bf16[128,2,256,256]{3,2,1,0:T(8,128)(2,1)} custom-call(s32[1]{0:T(128)} %bitcast.first_ref, s32[256,256]{1,0:T(8,128)S(1)} %bitcast.2), custom_call_target="tpu_custom_call" | custom-call | flops 503316480 | bytes 33554432 | tf_op jit(solution)/shard_map/weights/pallas_call | solution.py:225
  71.3 11.3 %all-to-all-done.g_ref = bf16[16,160,256]{2,1,0:T(8,128)(2,1)S(1)} async-done(((bf16[16,160,256]{2,1,0:T(8,128)(2,1)}), bf16[16,160,256]{2,1,0:T(8,128)(2,1)S(1)}, u32[]{:S(2)}, u32[]{:S(2)}) %all-to-all-start) | async-done | bytes 1310752 | tf_op jit(solution)/shard_map/all_to_all | solution.py:417
  82.6 5.2 %all-to-all-start.1 = ((bf16[16,96,256]{2,1,0:T(8,128)(2,1)}), bf16[16,96,256]{2,1,0:T(8,128)(2,1)S(1)}, u32[]{:S(2)}, u32[]{:S(2)}) async-start(bf16[16,96,256]{2,1,0:T(8,128)(2,1)} %get-tuple-element.15), calls=%async_computation.1 | async-start | bytes 1572864 | tf_op jit(solution)/shard_map/all_to_all | solution.py:417
  87.9 0.0 copy-done.3
  87.9 16.0 %combine.2 = (bf16[2,128,256,256]{3,2,1,0:T(8,128)(2,1)}, bf16[128,16,256]{2,1,0:T(8,128)(2,1)}) custom-call(bf16[16,160,256]{2,1,0:T(8,128)(2,1)S(1)} %all-to-all-done.g_ref, f32[2,128,256]{2,1,0:T(8,128)S(1)} %copy-done.3, bf16[128,2,256,256]{3,2,1,0:T(8,128)(2,1)} %weights.1.w_ref), custom_call_target="tpu_custom_call" | custom-call | flops 1342177280 | bytes 41943040 | tf_op jit(solution)/shard_map/combine/pallas_call | solution.py:346
  103.9 3.6 %all-to-all-done.1.g_ref = bf16[16,96,256]{2,1,0:T(8,128)(2,1)S(1)} async-done(((bf16[16,96,256]{2,1,0:T(8,128)(2,1)}), bf16[16,96,256]{2,1,0:T(8,128)(2,1)S(1)}, u32[]{:S(2)}, u32[]{:S(2)}) %all-to-all-start.1) | async-done | bytes 786464 | tf_op jit(solution)/shard_map/all_to_all | solution.py:417
  107.4 10.5 %combine.3 = (bf16[2,128,256,256]{3,2,1,0:T(8,128)(2,1)}, bf16[128,16,256]{2,1,0:T(8,128)(2,1)}) custom-call(bf16[16,96,256]{2,1,0:T(8,128)(2,1)S(1)} %all-to-all-done.1.g_ref, f32[2,128,256]{2,1,0:T(8,128)S(1)} %copy-done.3, bf16[128,2,256,256]{3,2,1,0:T(8,128)(2,1)} %weights.1.w_ref, ...), custom_call_target="tpu_custom_call", output_to_operand_aliasing={{0}: (3, {}), {1}: (4, {})} | custom-call | flops 805306368 | bytes 25165824 | tf_op jit(solution)/shard_map/combine/pallas_call | solution.py:346
  (1 shorter events, 0.0 us)
Async XLA Ops:
  0.6 28.9 %copy-start = (s32[64,16384]{1,0:T(8,128)S(1)}, s32[64,16384]{1,0:T(8,128)}, u32[]{:S(2)}) copy-start(s32[64,16384]{1,0:T(8,128)} %x_ref.3) | copy-start | bytes 12582916
  0.6 28.9 %copy-start.2 = (bf16[16,256,256]{2,1,0:T(8,128)(2,1)S(1)}, bf16[16,256,256]{2,1,0:T(8,128)(2,1)}, u32[]{:S(2)}) copy-start(bf16[16,256,256]{2,1,0:T(8,128)(2,1)} %constant.18.clone.refs_2_.refs_3_) | copy-start | bytes 6291460
  3.2 26.3 %copy-start.1 = (bf16[16,256,256]{2,1,0:T(8,128)(2,1)S(1)}, bf16[16,256,256]{2,1,0:T(8,128)(2,1)}, u32[]{:S(2)}) copy-start(bf16[16,256,256]{2,1,0:T(8,128)(2,1)} %constant.19.clone.refs_3_.refs_4_) | copy-start | bytes 6291460
  3.2 26.3 %copy-start.4 = (f32[4,4096]{1,0:T(4,128)S(1)}, f32[4,4096]{1,0:T(4,128)}, u32[]{:S(2)}) copy-start(f32[4,4096]{1,0:T(4,128)} %constant.17.clone.refs_1_.refs_2_) | copy-start | bytes 196612
  3.3 26.2 %collective-permute-start = (bf16[64,8192]{1,0:T(8,128)(2,1)S(1)}, bf16[64,8192]{1,0:T(8,128)(2,1)S(1)}, u32[]{:S(2)}, u32[]{:S(2)}) collective-permute-start(bf16[64,8192]{1,0:T(8,128)(2,1)S(1)} %slice.10), channel_id=1, source_target_pairs={{4,0},{8,4},{12,8},{5,1},{9,5},{13,9},{6,2},{10,6},{14,10},{7,3},{... | collective-permute-start | bytes 3145736 | tf_op jit(solution)/shard_map/ppermute | solution.py:34
  5.5 35.2 %collective-permute-start.1 = (bf16[64,4096]{1,0:T(8,128)(2,1)S(1)}, bf16[64,4096]{1,0:T(8,128)(2,1)S(1)}, u32[]{:S(2)}, u32[]{:S(2)}) collective-permute-start(bf16[64,4096]{1,0:T(8,128)(2,1)S(1)} %slice.11), channel_id=1, source_target_pairs={{4,0},{8,4},{12,8},{5,1},{9,5},{13,9},{6,2},{10,6},{14,10},{7,3},{... | collective-permute-start | bytes 1572872 | tf_op jit(solution)/shard_map/ppermute | solution.py:34
  45.9 6.6 %copy-start.5 = (s32[256,256]{1,0:T(8,128)S(1)}, s32[256,256]{1,0:T(8,128)}, u32[]{:S(2)}) copy-start(s32[256,256]{1,0:T(8,128)} %param.7) | copy-start | bytes 786436
  45.9 36.8 %all-to-all-start = ((bf16[16,160,256]{2,1,0:T(8,128)(2,1)}), bf16[16,160,256]{2,1,0:T(8,128)(2,1)S(1)}, u32[]{:S(2)}, u32[]{:S(2)}) async-start(bf16[16,160,256]{2,1,0:T(8,128)(2,1)} %get-tuple-element.14), calls=%async_computation | async-start | bytes 2621440 | tf_op jit(solution)/shard_map/all_to_all | solution.py:417
  52.6 35.3 %copy-start.3 = (f32[2,128,256]{2,1,0:T(8,128)S(1)}, f32[2,128,256]{2,1,0:T(8,128)}, u32[]{:S(2)}) copy-start(f32[2,128,256]{2,1,0:T(8,128)} %gain_ref.3) | copy-start | bytes 786436
  82.6 24.8 %all-to-all-start.1 = ((bf16[16,96,256]{2,1,0:T(8,128)(2,1)}), bf16[16,96,256]{2,1,0:T(8,128)(2,1)S(1)}, u32[]{:S(2)}, u32[]{:S(2)}) async-start(bf16[16,96,256]{2,1,0:T(8,128)(2,1)} %get-tuple-element.15), calls=%async_computation.1 | async-start | bytes 1572864 | tf_op jit(solution)/shard_map/all_to_all | solution.py:417

commit v4 on v3

--- a/solution.py
+++ b/solution.py
@@ -160,7 +160,7 @@
     lanes = inputs * blocks
     own = spec - half * blocks
     wanted = (blocks + TAPS - 1) * NFFT - own * NFFT
-    rows_in, pairs = 16, 4
+    rows_in, pairs = 32, 8
     steps_in, steps_out = inputs // rows_in, PAIRS // pairs
     unit = ROWS // owners // sum(SHARES)
     before = lambda g: jnp.minimum(g, steps_in - 1)
@@ -246,11 +246,11 @@
     before = sum(SHARES[:share]) * (GROUP // CHAN_BLOCK)
     slot = step % SLOTS
 
-    def vis_copies(at_step):
+    def vis_copies(at_step, pieces=range(COPIES)):
         at = at_step % SLOTS
         wide = CHAN_BLOCK // COPIES
         for part in range(2):
-            for c in range(COPIES):
+            for c in pieces:
                 yield pltpu.make_async_copy(
                     held.at[at, part, pl.ds(c * wide, wide)],
                     vis_ref.at[part, pl.ds((before + at_step) * CHAN_BLOCK + c * wide, wide)],
@@ -326,9 +326,10 @@
         formed = lax.dot_general(left, w, (((1,), (0,)), ((), ())), preferred_element_type=jnp.float32)
         formed = formed * formed
         power_ref[u] = (formed[:times] + formed[times:]).astype(jnp.bfloat16)
-
-    for copy in vis_copies(step):
-        copy.start()
+        if (u + 1) % (CHAN_BLOCK // COPIES) == 0:
+            for copy in vis_copies(step, [u // (CHAN_BLOCK // COPIES)]):
+                copy.start()
+
 
     @pl.when(step == steps - 1)
     def _():
@@ -400,8 +401,9 @@
     owners = tm_count * chan_count
     chan_local = CH // owners
     spec_dev = voltages.shape[1] // NFFT
-    early = shifted(voltages[:, : 2 * NFFT].astype(jnp.bfloat16), "tm", -1)
-    late = shifted(voltages[:, 2 * NFFT : (TAPS - 1) * NFFT].astype(jnp.bfloat16), "tm", -1)
+    head = lax.optimization_barrier(voltages[:, : (TAPS - 1) * NFFT].astype(jnp.bfloat16))
+    early = shifted(head[:, : 2 * NFFT], "tm", -1)
+    late = shifted(head[:, 2 * NFFT :], "tm", -1)
     chan_first = (lax.axis_index("tm") * chan_count + lax.axis_index("chan")) * chan_local
     weights = beam_weights(beam_delays, chan_first, chan_local)
     tables = [jnp.asarray(table) for table in (window_table(), *second_tables())]

time: 118 us -> 117 us (level)
  local copies, waits for them, and re-layouts: 0.27 us -> 1.85 us
    unnamed x13, local copies, waits for them, and re-layouts: 0.16 us -> 1.74 us
where the time goes in v4:
time: 117 us
  Pallas kernels  54.3 us (46%)
  waiting for transfers between devices  42 us (36%)
  starting transfers between devices  15.8 us (14%)
  other arithmetic  2.2 us (2%)
  local copies, waits for them, and re-layouts  1.85 us (2%)
    ppermute x2, waiting for transfers between devices, shifted(): return lax.ppermute(block, axis, route)  27.1 us
    pallas_call x2, Pallas kernels, combine(): pl.pallas_call(functools.partial(combine_kernel, tm_count, spec, inputs,...  26.4 us
    pallas_call x1, Pallas kernels, beam_weights(): pl.pallas_call(functools.partial(weights_kernel, 1.0 / math.sqrt(inputs))...  18.7 us
    all_to_all x2, waiting for transfers between devices, shards(): lax.all_to_all(block, ('tm', 'chan'), split_axis=0, concat_axis=0, tiled=...  14.9 us
    all_to_all x2, starting transfers between devices, shards(): lax.all_to_all(block, ('tm', 'chan'), split_axis=0, concat_axis=0, tiled=...  11.8 us
    pallas_call x2, Pallas kernels, spectra(): pl.pallas_call(functools.partial(spectra_kernel, half, blocks, rows_in, s...  9.17 us
    ppermute x2, starting transfers between devices, shifted(): return lax.ppermute(block, axis, route)  3.97 us
  transfers between devices with their start and end apart: 4, of which 4 were waited for; matrix products, arithmetic and copies ran while one was open for 0% of the time, Pallas kernels for 34%

profile of v4, /device:TPU:9, one launch (start us, length us, event | category | flops | bytes accessed | tf_op | source)
XLA Modules:
  0.0 116.9 jit_solution(8973182410051167098)
XLA Ops:
  0.6 0.0 copy-start
  0.6 2.2 %slice_convert_fusion = bf16[64,12288]{1,0:T(8,128)(2,1)S(1)} fusion(s32[64,16384]{1,0:T(8,128)} %x_ref.3), kind=kLoop, calls=%fused_computation | loop fusion | flops 786432 | bytes 4718592 | tf_op jit(solution)/shard_map/convert
  2.8 0.0 copy-start.1
  2.9 0.0 copy-start.4
  2.9 0.1 slice.14
  2.9 2.1 %collective-permute-start = (bf16[64,8192]{1,0:T(8,128)(2,1)S(1)}, bf16[64,8192]{1,0:T(8,128)(2,1)S(1)}, u32[]{:S(2)}, u32[]{:S(2)}) collective-permute-start(bf16[64,8192]{1,0:T(8,128)(2,1)S(1)} %slice.14), channel_id=1, source_target_pairs={{4,0},{8,4},{12,8},{5,1},{9,5},{13,9},{6,2},{10,6},{14,10},{7,3},{... | collective-permute-start | bytes 3145736 | tf_op jit(solution)/shard_map/ppermute | solution.py:34
  5.0 1.9 %collective-permute-start.1 = (bf16[64,4096]{1,0:T(8,128)(2,1)S(1)}, bf16[64,4096]{1,0:T(8,128)(2,1)S(1)}, u32[]{:S(2)}, u32[]{:S(2)}) collective-permute-start(bf16[64,4096]{1,0:T(8,128)(2,1)S(1)} %slice.15), channel_id=1, source_target_pairs={{4,0},{8,4},{12,8},{5,1},{9,5},{13,9},{6,2},{10,6},{14,10},{7,3},{... | collective-permute-start | bytes 1572872 | tf_op jit(solution)/shard_map/ppermute | solution.py:34
  7.0 22.0 %collective-permute-done.refs_0_ = bf16[64,8192]{1,0:T(8,128)(2,1)S(1)} collective-permute-done((bf16[64,8192]{1,0:T(8,128)(2,1)S(1)}, bf16[64,8192]{1,0:T(8,128)(2,1)S(1)}, u32[]{:S(2)}, u32[]{:S(2)}) %collective-permute-start) | collective-permute-done | bytes 1048608 | tf_op jit(solution)/shard_map/ppermute | solution.py:34
  29.0 0.0 copy-done
  29.0 0.0 copy-done.1
  29.0 0.0 copy-done.4
  29.0 0.0 copy-start.2
  29.0 1.6 %copy-done.2 = bf16[16,256,256]{2,1,0:T(8,128)(2,1)S(1)} copy-done((bf16[16,256,256]{2,1,0:T(8,128)(2,1)S(1)}, bf16[16,256,256]{2,1,0:T(8,128)(2,1)}, u32[]{:S(2)}) %copy-start.2) | copy-done | bytes 2097176
  30.6 4.5 %spectra.2 = (bf16[16,160,256]{2,1,0:T(8,128)(2,1)}, bf16[16,96,256]{2,1,0:T(8,128)(2,1)}) custom-call(s32[64,16384]{1,0:T(8,128)S(1)} %copy-done, bf16[64,8192]{1,0:T(8,128)(2,1)S(1)} %collective-permute-done.refs_0_, f32[4,4096]{1,0:T(4,128)S(1)} %copy-done.4, bf16[16,256,256]{2,1,0:T(8,128)(2,1)S(1)} %copy-done.2, bf16[16,256,256]{2,1,0:T(8,128)(2,1)S(1)} %copy-done.1), custom_call_target="tpu_custom_call" | custom-call | flops 805306368 | bytes 8388608 | tf_op jit(solution)/shard_map/spectra/pallas_call | solution.py:168
  35.1 5.1 %collective-permute-done.1.refs_1_ = bf16[64,4096]{1,0:T(8,128)(2,1)S(1)} collective-permute-done((bf16[64,4096]{1,0:T(8,128)(2,1)S(1)}, bf16[64,4096]{1,0:T(8,128)(2,1)S(1)}, u32[]{:S(2)}, u32[]{:S(2)}) %collective-permute-start.1) | collective-permute-done | bytes 524320 | tf_op jit(solution)/shard_map/ppermute | solution.py:34
  40.2 4.7 %spectra.3 = (bf16[16,160,256]{2,1,0:T(8,128)(2,1)}, bf16[16,96,256]{2,1,0:T(8,128)(2,1)}) custom-call(s32[64,16384]{1,0:T(8,128)S(1)} %copy-done, bf16[64,8192]{1,0:T(8,128)(2,1)S(1)} %collective-permute-done.refs_0_, bf16[64,4096]{1,0:T(8,128)(2,1)S(1)} %collective-permute-done.1.refs_1_, ...), custom_call_target="tpu_custom_call", output_to_operand_aliasing={{0}: (6, {}), {1}: (7, {})} | custom-call | flops 805306368 | bytes 8388608 | tf_op jit(solution)/shard_map/spectra/pallas_call | solution.py:168
  44.9 0.0 copy-start.5
  44.9 6.6 %all-to-all-start = ((bf16[16,160,256]{2,1,0:T(8,128)(2,1)}), bf16[16,160,256]{2,1,0:T(8,128)(2,1)S(1)}, u32[]{:S(2)}, u32[]{:S(2)}) async-start(bf16[16,160,256]{2,1,0:T(8,128)(2,1)} %get-tuple-element.14), calls=%async_computation | async-start | bytes 2621440 | tf_op jit(solution)/shard_map/all_to_all | solution.py:419
  51.5 0.0 copy-done.5
  51.5 0.1 copy.12
  51.6 0.0 copy-start.3
  51.6 18.7 %weights.1.w_ref = bf16[128,2,256,256]{3,2,1,0:T(8,128)(2,1)} custom-call(s32[1]{0:T(128)} %bitcast.first_ref, s32[256,256]{1,0:T(8,128)S(1)} %bitcast.2), custom_call_target="tpu_custom_call" | custom-call | flops 503316480 | bytes 33554432 | tf_op jit(solution)/shard_map/weights/pallas_call | solution.py:225
  70.4 11.3 %all-to-all-done.g_ref = bf16[16,160,256]{2,1,0:T(8,128)(2,1)S(1)} async-done(((bf16[16,160,256]{2,1,0:T(8,128)(2,1)}), bf16[16,160,256]{2,1,0:T(8,128)(2,1)S(1)}, u32[]{:S(2)}, u32[]{:S(2)}) %all-to-all-start) | async-done | bytes 1310752 | tf_op jit(solution)/shard_map/all_to_all | solution.py:419
  81.6 5.2 %all-to-all-start.1 = ((bf16[16,96,256]{2,1,0:T(8,128)(2,1)}), bf16[16,96,256]{2,1,0:T(8,128)(2,1)S(1)}, u32[]{:S(2)}, u32[]{:S(2)}) async-start(bf16[16,96,256]{2,1,0:T(8,128)(2,1)} %get-tuple-element.15), calls=%async_computation.1 | async-start | bytes 1572864 | tf_op jit(solution)/shard_map/all_to_all | solution.py:419
  86.9 0.0 copy-done.3
  86.9 16.0 %combine.2 = (bf16[2,128,256,256]{3,2,1,0:T(8,128)(2,1)}, bf16[128,16,256]{2,1,0:T(8,128)(2,1)}) custom-call(bf16[16,160,256]{2,1,0:T(8,128)(2,1)S(1)} %all-to-all-done.g_ref, f32[2,128,256]{2,1,0:T(8,128)S(1)} %copy-done.3, bf16[128,2,256,256]{3,2,1,0:T(8,128)(2,1)} %weights.1.w_ref), custom_call_target="tpu_custom_call" | custom-call | flops 1342177280 | bytes 41943040 | tf_op jit(solution)/shard_map/combine/pallas_call | solution.py:347
  102.9 3.6 %all-to-all-done.1.g_ref = bf16[16,96,256]{2,1,0:T(8,128)(2,1)S(1)} async-done(((bf16[16,96,256]{2,1,0:T(8,128)(2,1)}), bf16[16,96,256]{2,1,0:T(8,128)(2,1)S(1)}, u32[]{:S(2)}, u32[]{:S(2)}) %all-to-all-start.1) | async-done | bytes 786464 | tf_op jit(solution)/shard_map/all_to_all | solution.py:419
  106.5 10.5 %combine.3 = (bf16[2,128,256,256]{3,2,1,0:T(8,128)(2,1)}, bf16[128,16,256]{2,1,0:T(8,128)(2,1)}) custom-call(bf16[16,96,256]{2,1,0:T(8,128)(2,1)S(1)} %all-to-all-done.1.g_ref, f32[2,128,256]{2,1,0:T(8,128)S(1)} %copy-done.3, bf16[128,2,256,256]{3,2,1,0:T(8,128)(2,1)} %weights.1.w_ref, ...), custom_call_target="tpu_custom_call", output_to_operand_aliasing={{0}: (3, {}), {1}: (4, {})} | custom-call | flops 805306368 | bytes 25165824 | tf_op jit(solution)/shard_map/combine/pallas_call | solution.py:347
  (1 shorter events, 0.0 us)
Async XLA Ops:
  0.6 28.4 %copy-start = (s32[64,16384]{1,0:T(8,128)S(1)}, s32[64,16384]{1,0:T(8,128)}, u32[]{:S(2)}) copy-start(s32[64,16384]{1,0:T(8,128)} %x_ref.3) | copy-start | bytes 12582916
  2.8 26.2 %copy-start.1 = (bf16[16,256,256]{2,1,0:T(8,128)(2,1)S(1)}, bf16[16,256,256]{2,1,0:T(8,128)(2,1)}, u32[]{:S(2)}) copy-start(bf16[16,256,256]{2,1,0:T(8,128)(2,1)} %constant.19.clone.refs_3_.refs_4_) | copy-start | bytes 6291460
  2.9 26.2 %copy-start.4 = (f32[4,4096]{1,0:T(4,128)S(1)}, f32[4,4096]{1,0:T(4,128)}, u32[]{:S(2)}) copy-start(f32[4,4096]{1,0:T(4,128)} %constant.17.clone.refs_1_.refs_2_) | copy-start | bytes 196612
  2.9 26.1 %collective-permute-start = (bf16[64,8192]{1,0:T(8,128)(2,1)S(1)}, bf16[64,8192]{1,0:T(8,128)(2,1)S(1)}, u32[]{:S(2)}, u32[]{:S(2)}) collective-permute-start(bf16[64,8192]{1,0:T(8,128)(2,1)S(1)} %slice.14), channel_id=1, source_target_pairs={{4,0},{8,4},{12,8},{5,1},{9,5},{13,9},{6,2},{10,6},{14,10},{7,3},{... | collective-permute-start | bytes 3145736 | tf_op jit(solution)/shard_map/ppermute | solution.py:34
  5.0 35.2 %collective-permute-start.1 = (bf16[64,4096]{1,0:T(8,128)(2,1)S(1)}, bf16[64,4096]{1,0:T(8,128)(2,1)S(1)}, u32[]{:S(2)}, u32[]{:S(2)}) collective-permute-start(bf16[64,4096]{1,0:T(8,128)(2,1)S(1)} %slice.15), channel_id=1, source_target_pairs={{4,0},{8,4},{12,8},{5,1},{9,5},{13,9},{6,2},{10,6},{14,10},{7,3},{... | collective-permute-start | bytes 1572872 | tf_op jit(solution)/shard_map/ppermute | solution.py:34
  29.0 1.6 %copy-start.2 = (bf16[16,256,256]{2,1,0:T(8,128)(2,1)S(1)}, bf16[16,256,256]{2,1,0:T(8,128)(2,1)}, u32[]{:S(2)}) copy-start(bf16[16,256,256]{2,1,0:T(8,128)(2,1)} %constant.18.clone.refs_2_.refs_3_) | copy-start | bytes 6291460
  44.9 6.6 %copy-start.5 = (s32[256,256]{1,0:T(8,128)S(1)}, s32[256,256]{1,0:T(8,128)}, u32[]{:S(2)}) copy-start(s32[256,256]{1,0:T(8,128)} %param.7) | copy-start | bytes 786436
  44.9 36.8 %all-to-all-start = ((bf16[16,160,256]{2,1,0:T(8,128)(2,1)}), bf16[16,160,256]{2,1,0:T(8,128)(2,1)S(1)}, u32[]{:S(2)}, u32[]{:S(2)}) async-start(bf16[16,160,256]{2,1,0:T(8,128)(2,1)} %get-tuple-element.14), calls=%async_computation | async-start | bytes 2621440 | tf_op jit(solution)/shard_map/all_to_all | solution.py:419
  51.6 35.3 %copy-start.3 = (f32[2,128,256]{2,1,0:T(8,128)S(1)}, f32[2,128,256]{2,1,0:T(8,128)}, u32[]{:S(2)}) copy-start(f32[2,128,256]{2,1,0:T(8,128)} %gain_ref.3) | copy-start | bytes 786436
  81.6 24.8 %all-to-all-start.1 = ((bf16[16,96,256]{2,1,0:T(8,128)(2,1)}), bf16[16,96,256]{2,1,0:T(8,128)(2,1)S(1)}, u32[]{:S(2)}, u32[]{:S(2)}) async-start(bf16[16,96,256]{2,1,0:T(8,128)(2,1)} %get-tuple-element.15), calls=%async_computation.1 | async-start | bytes 1572864 | tf_op jit(solution)/shard_map/all_to_all | solution.py:419
